TPU v7x, 256 devices: a whole 4x4x8 slice. The times are simulated.
256 devices in a mesh: branch: 4 (over y_lo, core), dp: 16 (over z, y_hi), mp: 4 (over x).
Axes of the slice: x: 4, y: 4 (y_hi: 2, y_lo: 2; y = y_hi * 2 + y_lo), z: 8, core: 2. Of those that a mesh axis runs over, the one named last changes fastest.
Arguments:
- context: bfloat16 [8192, 4096], P(('branch', 'dp')), may hold values from -6 to 6
- residual: bfloat16 [8192, 4096], P(('branch', 'dp')), may hold values from -40 to 40
- branch_out_proj: bfloat16 [4, 4096, 4096], P('branch', 'dp', 'mp'), may hold values from -0.09375 to 0.09375
- norm_gain: bfloat16 [4096], replicated, may hold values from 0.25 to 1.75
- router: bfloat16 [4096, 4], replicated, may hold values from -0.09375 to 0.09375
- expert_ids: int32 [8192, 2], P(('branch', 'dp')), may hold values from 0 to 3, all different within a row; in each aligned block of 128 rows (0 to 127, 128 to 255, ...) at most 72 rows name the same one
- gate_proj: bfloat16 [4, 4096, 6144], P('branch', None, 'dp'), may hold values from -0.09375 to 0.09375
- up_proj: bfloat16 [4, 4096, 6144], P('branch', None, 'dp'), may hold values from -0.09375 to 0.09375
- down_proj: bfloat16 [4, 6144, 4096], P('branch', 'dp'), may hold values from -0.078125 to 0.078125
Outputs:
- mixed: bfloat16 [8192, 4096], P(('branch', 'dp'))
Inputs may be any that keep to these rules, and one draw needn't show every extreme that they name: `expert_ids`: among the rows of one device (aligned blocks of 128 rows), no expert is named by more than 72 rows; in some device one expert is named by exactly 72. A row names two different experts.
All inputs are finite; a program needn't handle non-finite values.
Results may differ from a plain program's by a relative error of at most 0.009.
Values may be sent and summed in bfloat16 or wider, within the bound.
A program may use at most 128 MiB of HBM per device.

v0:
```python
import jax
import jax.numpy as jnp
from jax import lax
from jax.sharding import PartitionSpec as P

CAP = 72


def local(
    context, residual, branch_out_proj, norm_gain, router, expert_ids, gate_proj, up_proj, down_proj
):
    branch_count = lax.axis_size("branch")
    lane_count = lax.axis_size("mp")
    own_block = branch_out_proj[0].astype(jnp.float32)
    summed_proj = lax.psum(own_block.astype(jnp.bfloat16), "branch").astype(jnp.float32)
    merged = (summed_proj / branch_count).astype(jnp.bfloat16)
    head_cols = lax.all_gather(merged, "dp", axis=0, tiled=True)
    col_part = jnp.dot(context, head_cols, preferred_element_type=jnp.float32)
    projected = lax.all_gather(col_part.astype(jnp.bfloat16), "mp", axis=1, tiled=True).astype(
        col_part.dtype
    )
    row_count = residual.shape[0]
    feature_count = residual.shape[1]
    hidden_state = residual.astype(jnp.float32) + projected
    inv_rms = lax.rsqrt(jnp.mean(hidden_state * hidden_state, axis=-1, keepdims=True) + 1e-05)
    normed = (hidden_state * inv_rms * norm_gain.astype(jnp.float32)).astype(jnp.bfloat16)
    logits = jnp.dot(normed, router, preferred_element_type=jnp.float32)
    scores = jax.nn.sigmoid(logits)
    expert_range = jnp.arange(branch_count, dtype=jnp.int32)
    chosen = (expert_ids[:, :, None] == expert_range[None, None, :]).astype(jnp.float32)
    selected = jnp.sum(chosen * scores[:, None, :], axis=-1)
    gate_weights = selected / jnp.sum(selected, axis=-1, keepdims=True)
    flat_ids = expert_ids.reshape(row_count * 2)
    one_hot = (flat_ids[:, None] == expert_range[None, :]).astype(jnp.int32)
    before = jnp.cumsum(one_hot, axis=0) - one_hot
    slot_index = jnp.sum(before * one_hot, axis=-1)
    target = flat_ids * CAP + slot_index
    slot_total = branch_count * CAP
    dispatch = (target[:, None] == jnp.arange(slot_total, dtype=jnp.int32)[None, :]).astype(
        jnp.bfloat16
    )
    dispatch = dispatch.reshape(row_count, 2, branch_count, CAP)
    cap_lane = CAP // lane_count
    lane_first = lax.axis_index("mp") * cap_lane
    lane_dispatch = lax.dynamic_slice_in_dim(dispatch, lane_first, cap_lane, 3)
    lane_dispatch = lane_dispatch.reshape(row_count, 2, branch_count * cap_lane)
    buffer = jnp.einsum(
        "tkq,td->qd", lane_dispatch, normed, preferred_element_type=jnp.float32
    ).astype(jnp.bfloat16)
    sent_tokens = lax.all_to_all(
        buffer.reshape(branch_count, cap_lane, feature_count),
        "branch",
        split_axis=0,
        concat_axis=0,
        tiled=True,
    )
    arrived = sent_tokens.reshape(branch_count * cap_lane, feature_count)
    shard_rows = lax.all_gather(arrived, "dp", axis=0, tiled=True)
    gate_act = jnp.dot(shard_rows, gate_proj[0], preferred_element_type=jnp.float32)
    up_act = jnp.dot(shard_rows, up_proj[0], preferred_element_type=jnp.float32)
    hidden_act = (jax.nn.silu(gate_act) * up_act).astype(jnp.bfloat16)
    block_terms = jnp.dot(hidden_act, down_proj[0], preferred_element_type=jnp.float32)
    expert_out = lax.psum_scatter(
        block_terms.astype(jnp.bfloat16), "dp", scatter_dimension=0, tiled=True
    )
    returned_out = lax.all_to_all(
        expert_out.reshape(branch_count, cap_lane, feature_count),
        "branch",
        split_axis=0,
        concat_axis=0,
        tiled=True,
    )
    all_slots = lax.all_gather(returned_out, "mp", axis=1, tiled=True)
    picked = jnp.einsum(
        "tkq,qd->tkd",
        dispatch.reshape(row_count, 2, slot_total),
        all_slots.reshape(slot_total, feature_count),
        preferred_element_type=jnp.float32,
    )
    mixed = hidden_state + jnp.sum(gate_weights[:, :, None] * picked, axis=1)
    return mixed.astype(jnp.bfloat16)


def solution(mesh):
    placed = (
        P(("branch", "dp"), None),
        P(("branch", "dp"), None),
        P("branch", "dp", "mp"),
        P(),
        P(),
        P(("branch", "dp"), None),
        P("branch", None, "dp"),
        P("branch", None, "dp"),
        P("branch", "dp", None),
    )
    return jax.shard_map(
        local, mesh=mesh, in_specs=placed, out_specs=P(("branch", "dp"), None), check_vma=False
    )
```

profile of v0, /device:TPU:8, one launch (start us, length us, event | category | flops | bytes accessed | tf_op | source)
XLA Modules:
  0.0 724.0 jit_solution(6917433802297792406)
XLA Ops:
  6.5 0.7 all-reduce.2.cloned.1.call-update
  7.3 0.0 all-gather.5.cloned.1.call-start
  7.3 47.7 %all-reduce.2.cloned.1.call-done = bf16[256,1024]{1,0:T(8,128)(2,1)} async-done(((bf16[256,1024]{1,0:T(8,128)(2,1)}), bf16[256,1024]{1,0:T(8,128)(2,1)}) %all-reduce.2.cloned.1.call-update) | async-done | bytes 524304 | tf_op jit(solution)/shard_map/psum | solution.py:15
  55.0 1.9 multiply_convert_fusion.1
  56.9 0.0 all-gather.5.cloned.1.call-update
  57.0 0.0 copy-start.3
  57.0 0.0 all-gather.7.cloned.1.call-start
  57.0 137.2 %all-gather.5.cloned.1.call-done = bf16[4096,1024]{1,0:T(8,128)(2,1)} async-done(((bf16[256,1024]{1,0:T(8,128)(2,1)}), bf16[4096,1024]{1,0:T(8,128)(2,1)}) %all-gather.5.cloned.1.call-update) | async-done | bytes 8388624 | tf_op jit(solution)/shard_map/all_gather | solution.py:17
  194.2 6.7 fusion.15
  200.9 0.0 all-gather.7.cloned.1.call-update
  201.0 0.0 all-gather.9.cloned.1.call-start
  201.0 0.1 copy.57
  201.1 0.1 eq.87
  201.3 0.1 eq.83
  201.5 1.2 reduce-window.6
  202.7 0.1 slice.8
  202.8 0.1 copy.59
  202.9 0.1 copy.60
  203.0 0.1 add_bitcast_fusion
  203.1 0.1 reduce_sum.62
  203.2 0.1 copy.61
  203.4 0.1 convert_reduce_fusion
  203.5 2.3 copy.56
  205.8 19.6 %all-gather.7.cloned.1.call-done = bf16[128,4096]{0,1:T(8,128)(2,1)} async-done(((bf16[128,1024]{0,1:T(8,128)(2,1)}), bf16[128,4096]{0,1:T(8,128)(2,1)}) %all-gather.7.cloned.1.call-update) | async-done | bytes 1048592 | tf_op jit(solution)/shard_map/all_gather | solution.py:19
  225.3 2.2 multiply_reduce_fusion
  227.6 1.8 convolution_convert_fusion.1
  229.4 2.1 reshape.107
  231.5 14.8 %all_to_all.10 = bf16[4,18,4096]{2,1,0:T(8,128)(2,1)} all-to-all(bf16[4,18,4096]{2,1,0:T(8,128)(2,1)} %reshape.107), channel_id=1, replica_groups=mesh['branch'=4,'dp'=16,'mp'=4] {'branch'}, dimensions={0} | all-to-all | bytes 1179648 | tf_op jit(solution)/shard_map/all_to_all | solution.py:50
  246.3 2.1 reshape.108
  248.4 0.0 all-gather.9.cloned.1.call-update
  248.4 0.0 reduce-scatter.2.cloned.1.call-start
  248.5 147.0 %all-gather.9.cloned.1.call-done = bf16[1152,4096]{1,0:T(8,128)(2,1)} async-done(((bf16[72,4096]{1,0:T(8,128)(2,1)}), bf16[1152,4096]{1,0:T(8,128)(2,1)}) %all-gather.9.cloned.1.call-update) | async-done | bytes 9437200 | tf_op jit(solution)/shard_map/all_gather | solution.py:58
  395.5 9.5 %fusion.2 = f32[1152,384]{1,0:T(8,128)} fusion(bf16[1152,4096]{1,0:T(8,128)(2,1)} %all-gather.9.cloned.1.call-done, bf16[1,4096,384]{2,1,0:T(8,128)(2,1)} %param.15), kind=kOutput, calls=%fused_computation.6 | convolution fusion | flops 3623878656 | bytes 14352384 | tf_op jit(solution)/shard_map/dot_general | solution.py:59
  405.0 15.9 %convolution_convert_fusion = bf16[1152,4096]{1,0:T(8,128)(2,1)} fusion(bf16[1,384,4096]{2,1,0:T(8,128)(2,1)S(1)} %copy-done, bf16[1152,4096]{1,0:T(8,128)(2,1)} %all-gather.9.cloned.1.call-done, bf16[1,4096,384]{2,1,0:T(8,128)(2,1)} %param.16, f32[1152,384]{1,0:T(8,128)} %fusion.2), kind=kOutput, calls=%fused_computation | convolution fusion | flops 7255130112 | bytes 26935296 | tf_op jit(solution)/shard_map/dot_general | solution.py:62
  420.8 0.0 reduce-scatter.2.cloned.1.call-update
  420.9 0.0 all-gather.11.cloned.1.call-start
  420.9 229.0 %reduce-scatter.2.cloned.1.call-done = bf16[72,4096]{1,0:T(8,128)(2,1)} async-done(((bf16[1152,4096]{1,0:T(8,128)(2,1)}), bf16[72,4096]{1,0:T(8,128)(2,1)}) %reduce-scatter.2.cloned.1.call-update) | async-done | bytes 589840 | tf_op jit(solution)/shard_map/reduce_scatter | solution.py:63
  649.9 2.1 reshape.109
  652.0 15.0 %all_to_all.11 = bf16[4,18,4096]{2,1,0:T(8,128)(2,1)S(1)} all-to-all(bf16[4,18,4096]{2,1,0:T(8,128)(2,1)} %reshape.109), channel_id=1, replica_groups=mesh['branch'=4,'dp'=16,'mp'=4] {'branch'}, dimensions={0} | all-to-all | bytes 1179648 | tf_op jit(solution)/shard_map/all_to_all | solution.py:66
  667.0 1.3 copy.63
  668.3 0.0 all-gather.11.cloned.1.call-update
  668.4 2.1 fusion.18
  670.5 32.4 %all-gather.11.cloned.1.call-done = bf16[4,72,4096]{2,0,1:T(4,128)(2,1)} async-done(((bf16[4,18,4096]{2,0,1:T(4,128)(2,1)}), bf16[4,72,4096]{2,0,1:T(4,128)(2,1)}) %all-gather.11.cloned.1.call-update) | async-done | bytes 2359312 | tf_op jit(solution)/shard_map/all_gather | solution.py:73
  702.9 3.0 copy.64
  705.9 2.6 fusion.9
  708.5 2.9 copy.65
  711.4 3.5 add_convert_fusion
  714.9 2.3 copy.66
  (25 shorter events, 0.2 us)
Async XLA Ops:
  6.5 398.4 %copy-start = (bf16[1,384,4096]{2,1,0:T(8,128)(2,1)S(1)}, bf16[1,384,4096]{2,1,0:T(8,128)(2,1)}, u32[]{:S(2)}) copy-start(bf16[1,384,4096]{2,1,0:T(8,128)(2,1)} %param.17) | copy-start | bytes 9437188
  6.5 48.4 %all-reduce.2.cloned.1.call-start = ((), (), s32[]{:S(2)}) async-start(), calls=%async_computation.3 | async-start | bytes 1048576 | tf_op jit(solution)/shard_map/psum | solution.py:15
  7.3 187.0 %all-gather.5.cloned.1.call-start = ((), (), s32[]{:S(2)}) async-start(), calls=%async_computation.4 | async-start | bytes 8912896 | tf_op jit(solution)/shard_map/all_gather | solution.py:17
  57.0 144.1 %copy-start.3 = (s32[128,2]{0,1:T(2,128)S(1)}, s32[128,2]{0,1:T(2,128)}, u32[]{:S(2)}) copy-start(s32[128,2]{0,1:T(2,128)} %param.14) | copy-start | bytes 3076
  57.0 144.5 %copy-start.4 = (bf16[4096]{0:T(1024)(128)(2,1)S(1)}, bf16[4096]{0:T(1024)(128)(2,1)}, u32[]{:S(2)}) copy-start(bf16[4096]{0:T(1024)(128)(2,1)} %param.12) | copy-start | bytes 24580
  57.0 168.4 %all-gather.7.cloned.1.call-start = ((), (), s32[]{:S(2)}) async-start(), calls=%async_computation.5 | async-start | bytes 1310720 | tf_op jit(solution)/shard_map/all_gather | solution.py:19
  201.0 194.6 %all-gather.9.cloned.1.call-start = ((), (), s32[]{:S(2)}) async-start(), calls=%async_computation.6 | async-start | bytes 10027008 | tf_op jit(solution)/shard_map/all_gather | solution.py:58
  225.3 2.3 copy-start.1
  225.3 2.3 copy-start.2
  248.4 401.4 %reduce-scatter.2.cloned.1.call-start = ((), (), s32[]{:S(2)}) async-start(), calls=%async_computation.7 | async-start | bytes 10027008 | tf_op jit(solution)/shard_map/reduce_scatter | solution.py:63
  420.9 282.1 %all-gather.11.cloned.1.call-start = ((), (), s32[]{:S(2)}) async-start(), calls=%async_computation.8 | async-start | bytes 2949120 | tf_op jit(solution)/shard_map/all_gather | solution.py:73
  652.0 16.4 %copy-start.5 = (bf16[4096,4]{0,1:T(4,128)(2,1)S(1)}, bf16[4096,4]{0,1:T(4,128)(2,1)}, u32[]{:S(2)}) copy-start(bf16[4096,4]{0,1:T(4,128)(2,1)} %param.13) | copy-start | bytes 98308
Sparse Core Ops, SparseCore 0:
  10.0 44.9 all-reduce.1
  57.6 136.6 all-gather.4
  201.1 24.2 all-gather.6
  248.6 146.8 all-gather.8
  421.0 228.8 reduce-scatter.1
  668.5 34.4 all-gather.10
where the time goes:
time: 726 us; the launch traced here: 724 us
  waiting for transfers between devices  614 us (85%)
  matrix products  38.6 us (5%)
  blocking collectives  29.8 us (4%)
  local copies, waits for them, and re-layouts  19 us (3%)
  between operations  13.6 us (2%)
  other arithmetic  9.21 us (1%)
    reduce_scatter x1, waiting for transfers between devices, local(): lax.psum_scatter(block_terms.astype(jnp.bfloat16), 'dp', scatter_dimensio...  229 us
    all_gather x1, waiting for transfers between devices, local(): shard_rows = lax.all_gather(arrived, 'dp', axis=0, tiled=True)  147 us
    all_gather x1, waiting for transfers between devices, local(): head_cols = lax.all_gather(merged, 'dp', axis=0, tiled=True)  137 us
    psum x1, waiting for transfers between devices, local(): lax.psum(own_block.astype(jnp.bfloat16), 'branch').astype(jnp.float32)  47.7 us
    all_gather x1, waiting for transfers between devices, local(): all_slots = lax.all_gather(returned_out, 'mp', axis=1, tiled=True)  32.4 us
    all_gather x1, waiting for transfers between devices, local(): lax.all_gather(col_part.astype(jnp.bfloat16), 'mp', axis=1, tiled=True)  19.6 us
    dot_general x1, matrix products, local(): jnp.dot(hidden_act, down_proj[0], preferred_element_type=jnp.float32)  15.9 us
    all_to_all x1, blocking collectives, local(): lax.all_to_all(expert_out.reshape(branch_count, cap_lane, feature_count),...  15 us
  transfers between devices with their start and end apart: 6, of which 6 were waited for; matrix products, arithmetic and copies ran while one was open for 1% of the time, Pallas kernels for 0%

commit v1 on v0

v1 whole, which is shorter than its diff:
```python
import functools

import jax
import jax.numpy as jnp
from jax import lax
from jax.experimental import pallas as pl
from jax.experimental.pallas import tpu as pltpu
from jax.sharding import PartitionSpec as P

NX, NY, NZ = 4, 4, 8
MESH = pl.DeviceIdType.MESH
F32, BF16 = jnp.float32, jnp.bfloat16
GATES = 128


def position():
    b, d, x = lax.axis_index("branch"), lax.axis_index("dp"), lax.axis_index("mp")
    return x, (d % 2) * 2 + b // 2, d // 2, b % 2


def device(x, y, z, core):
    return {"branch": (y % 2) * 2 + core, "dp": z * 2 + y // 2, "mp": x}


def rows(start, size):
    return pl.ds(pl.multiple_of(start, size), size)


class Ring:
    def __init__(self, n, me, at, send, recv):
        self.n, self.me, self.at, self.send_sem, self.recv_sem = n, me, at, send, recv
        self.sent = []

    def near(self, step):
        return (self.me + step + self.n) % self.n

    def live(self, k, h, way):
        return k < self.n // 2 or h == way

    def lanes(self, k):
        return [(h, way) for h in (0, 1) for way in (0, 1) if self.live(k, h, way)]

    def copy(self, src, dst, k, h, way):
        return pltpu.make_async_remote_copy(
            src_ref=src,
            dst_ref=dst,
            send_sem=self.send_sem(way, k - 1, h),
            recv_sem=self.recv_sem(way, k - 1, h),
            device_id=self.at(self.near(1 if way == 0 else -1)),
            device_id_type=MESH,
        )

    def drain(self):
        for c in self.sent:
            c.wait_send()


class Gather(Ring):
    def __init__(self, n, me, at, send, recv, block):
        super().__init__(n, me, at, send, recv)
        self.block, self.seen = block, set()

    def start(self, k):
        for h, way in self.lanes(k):
            if k > 1:
                self.arrive(k - 1, h, way)
            part = self.block(self.near(1 - k if way == 0 else k - 1), h)
            c = self.copy(part, part, k, h, way)
            c.start()
            self.sent.append(c)

    def arrive(self, k, h, way):
        if (k, h, way) not in self.seen:
            self.seen.add((k, h, way))
            part = self.block(self.near(-k if way == 0 else k), h)
            self.copy(part, part, k, h, way).wait_recv()

    def arrived(self, k):
        for h, way in self.lanes(k):
            self.arrive(k, h, way)


class Scatter(Ring):
    def __init__(self, n, me, at, send, recv, block, landing):
        super().__init__(n, me, at, send, recv)
        self.block, self.landing = block, landing

    def live(self, k, h, way):
        return k > 1 or h == way

    def put(self, k, h, way):
        far = self.n // 2 - k + 1
        c = self.copy(
            self.block(self.near(far if way == 0 else -far), h), self.landing(way, k - 1, h), k, h, way
        )
        c.start()
        self.sent.append(c)

    def first(self):
        for h, way in self.lanes(1):
            self.put(1, h, way)
        for h in (0, 1):
            for way in (0, 1):
                if not self.live(1, h, way):
                    self.put(2, h, way)

    def advance(self, k):
        for h, way in self.lanes(k):
            arrived = self.landing(way, k - 1, h)
            self.copy(arrived, arrived, k, h, way).wait_recv()
            left = self.n // 2 - k
            mine = self.block(self.near(left if way == 0 else -left), h)
            mine[...] = (mine[...].astype(F32) + arrived[...].astype(F32)).astype(BF16)
            if left:
                self.put(k + 1, h, way)


def greet(peers):
    barrier = pltpu.get_barrier_semaphore()
    for peer in peers:
        pl.semaphore_signal(barrier, inc=1, device_id=peer, device_id_type=MESH)
    pl.semaphore_wait(barrier, len(peers))


def project_kernel(
    block_ref, context_ref, residual_ref, gain_ref, router_ref, ids_ref, gate_ref, up_ref, down_ref,
    token_ref, hidden_ref, gate_out, up_out, down_out,
    context_two, pieces, merged, total, part, parts,
    pair_send, pair_recv, ring_send, ring_recv, lane_send, lane_recv,
):
    x, y, z, core = position()
    other = 1 - core
    half = y % 2
    base = y - half
    mate = base + 1 - half
    peers = [device(x, y, z, other), device(x, mate, z, core), device(x, mate, z, other)]
    far_side = (y + 1 + 2 * (1 - half)) % NY
    peers += [device(x, far_side, z, core), device(x, y, (z + 1) % NZ, core), device(x, y, (z + 7) % NZ, core)]
    for dx in (1, 2, 3):
        for c in (core, other):
            peers.append(device((x + dx) % NX, y, z, c))
    greet(peers)

    def pair_copy(i, src, dst, to):
        return pltpu.make_async_remote_copy(
            src_ref=src, dst_ref=dst, send_sem=pair_send.at[i], recv_sem=pair_recv.at[i],
            device_id=to, device_id_type=MESH,
        )

    tall, wide = block_ref.shape[0] // 2, block_ref.shape[1] // 2
    pending = []
    for i, (dy, dc) in enumerate(((0, 1), (1, 0), (1, 1))):
        to_half = half if dy == 0 else 1 - half
        to_core = core if dc == 0 else other
        pending.append(pair_copy(
            i, block_ref.at[rows(to_half * tall, tall), rows(to_core * wide, wide)], pieces.at[i],
            device(x, base + to_half, z, to_core),
        ))
    sibling = device(x, y, z, other)
    pending.append(pair_copy(3, context_ref, context_two, sibling))
    pending.append(pair_copy(4, gate_ref, gate_out, sibling))
    pending.append(pair_copy(5, up_ref, up_out, sibling))
    pending.append(pair_copy(6, down_ref, down_out, sibling))
    for c in pending:
        c.start()
    for c in pending[:3]:
        c.wait_recv()
    own = block_ref[rows(half * tall, tall), rows(core * wide, wide)].astype(F32)
    own = own + pieces[0].astype(F32) + pieces[1].astype(F32) + pieces[2].astype(F32)
    merged[z, rows(y * tall, tall), :] = (own * 0.25).astype(BF16)

    quarter = wide // 2

    def ring_sems(i):
        return (lambda way, k, h: ring_send.at[i, way, k, h]), (lambda way, k, h: ring_recv.at[i, way, k, h])

    at_y = lambda p: device(x, p, z, core)
    at_z = lambda p: device(x, y, p, core)
    a_y = Gather(NY, y, at_y, *ring_sems(0), lambda i, h: merged.at[
        z, rows(i * tall + h * (tall // 2), tall // 2), pl.ds(0, quarter)])
    b_z = Gather(NZ, z, at_z, *ring_sems(1), lambda i, h: merged.at[
        i, rows(y * tall + h * (tall // 2), tall // 2), pl.ds(quarter, quarter)])
    a_z = Gather(NZ, z, at_z, *ring_sems(2), lambda i, h: merged.at[
        i, pl.ds(h * 2 * tall, 2 * tall), pl.ds(0, quarter)])
    b_y = Gather(NY, y, at_y, *ring_sems(3), lambda i, h: merged.at[
        pl.ds(h * 4, 4), rows(i * tall, tall), pl.ds(quarter, quarter)])
    gather_all(a_y, b_z, a_z, b_y, {})

    pending[3].wait_recv()
    total[...] = jnp.zeros_like(total)

    @pl.loop(0, NZ)
    def _(k):
        depth = rows(k * 4 * tall, 4 * tall)
        total[0] += jnp.dot(context_ref[:, depth], merged[k], preferred_element_type=F32)
        total[1] += jnp.dot(context_two[:, depth], merged[k], preferred_element_type=F32)

    part[...] = total[...].astype(BF16)
    few = residual_ref.shape[0] // NX
    parts[x * 2 + core] = part[0, rows(x * few, few), :]
    lanes = []
    for dx in range(NX):
        for dc in range(2):
            if dx or dc:
                to_x = (x + dx) % NX
                c = pltpu.make_async_remote_copy(
                    src_ref=part.at[dc, rows(to_x * few, few), :],
                    dst_ref=parts.at[x * 2 + core],
                    send_sem=lane_send.at[dx * 2 + dc], recv_sem=lane_recv.at[dx * 2 + dc],
                    device_id=device(to_x, y, z, core if dc == 0 else other), device_id_type=MESH,
                )
                c.start()
                lanes.append((dx, dc, c))
    for dx, dc, c in lanes:
        land = parts.at[(x + NX - dx) % NX * 2 + (core if dc == 0 else other)]
        pltpu.make_async_remote_copy(
            src_ref=land, dst_ref=land,
            send_sem=lane_send.at[dx * 2 + dc], recv_sem=lane_recv.at[dx * 2 + dc],
            device_id=sibling, device_id_type=MESH,
        ).wait_recv()
    here = rows(x * few, few)
    features = residual_ref.shape[1]
    squares = jnp.zeros((few, 1), F32)
    for j in range(2 * NX):
        columns = pl.ds(j * wide, wide)
        hidden = residual_ref[here, columns].astype(F32) + parts[j].astype(F32)
        hidden_ref[:, columns] = hidden
        squares = squares + jnp.sum(hidden * hidden, axis=-1, keepdims=True)
    inv_rms = lax.rsqrt(squares / features + 1e-05)
    logits = jnp.zeros((few, GATES), F32)
    for j in range(2 * NX):
        columns = pl.ds(j * wide, wide)
        normed = (hidden_ref[:, columns] * inv_rms * gain_ref[:, columns].astype(F32)).astype(BF16)
        token_ref[:, columns] = normed
        logits = logits + jnp.dot(normed, router_ref[columns, :], preferred_element_type=F32)
    scores = 1.0 / (1.0 + jnp.exp(-logits))
    lane = lax.broadcasted_iota(jnp.int32, (few, GATES), 1)
    expert = lane % 4
    ids = ids_ref[here, :]
    first, second = ids[:, 0:1] == expert, ids[:, 1:2] == expert
    once = lane < 4
    picked_first = jnp.sum(jnp.where(first & once, scores, 0.0), axis=-1, keepdims=True)
    picked_second = jnp.sum(jnp.where(second & once, scores, 0.0), axis=-1, keepdims=True)
    weight = jnp.where(first, picked_first, jnp.where(second, picked_second, 0.0))
    weight = weight / (picked_first + picked_second)
    high = weight.astype(BF16).astype(F32)
    mid = (weight - high).astype(BF16).astype(F32)
    low = weight - high - mid
    sent = jnp.where(lane < 4, high, jnp.where(lane < 8, mid, jnp.where(lane < 12, low, 0.0)))
    token_ref[:, pl.ds(features, GATES)] = sent.astype(BF16)

    for c in pending[4:]:
        c.wait_recv()
    for c in pending:
        c.wait_send()
    for ring in (a_y, b_z, a_z, b_y):
        ring.drain()
    for _, _, c in lanes:
        c.wait_send()


def gather_all(a_y, b_z, a_z, b_y, then):
    run = lambda name: then.get(name, lambda: None)()
    a_y.start(1)
    b_z.start(1)
    a_y.start(2)
    b_z.start(2)
    a_y.arrived(1)
    a_y.arrived(2)
    a_z.start(1)
    b_z.start(3)
    b_z.start(4)
    for k in (1, 2, 3, 4):
        b_z.arrived(k)
    b_y.start(1)
    run("a0")
    a_z.start(2)
    run("b0")
    a_z.arrived(1)
    run("a1")
    a_z.start(3)
    b_y.start(2)
    a_z.arrived(2)
    run("a2")
    a_z.start(4)
    b_y.arrived(1)
    run("b1")
    a_z.arrived(3)
    run("a3")
    b_y.arrived(2)
    run("b2")
    a_z.arrived(4)
    run("a4")


def expert_kernel(
    token_ref, hidden_ref, gate_own, up_own, down_own, gate_two, up_two, down_two,
    out_ref,
    tok_a, tok_b, enter, leave, act, inner, sum_a, sum_b, land_az, land_by, land_ay, land_bz, mixed,
    load_sem, ring_send, ring_recv, lane_send, lane_recv,
):
    x, y, z, core = position()
    peers = [device(x, (y + 1) % NY, z, core), device(x, (y + 3) % NY, z, core)]
    peers += [device(x, y, (z + 1) % NZ, core), device(x, y, (z + 7) % NZ, core)]
    peers += [device((x + dx) % NX, y, z, core) for dx in (1, 2, 3)]
    width = gate_own.shape[1]
    loads = []
    for i, (src, dst) in enumerate((
        (gate_own, enter.at[:, pl.ds(0, width)]),
        (up_own, enter.at[:, pl.ds(width, width)]),
        (gate_two, enter.at[:, pl.ds(2 * width, width)]),
        (up_two, enter.at[:, pl.ds(3 * width, width)]),
        (down_own, leave.at[pl.ds(0, width), :]),
        (down_two, leave.at[pl.ds(width, width), :]),
    )):
        c = pltpu.make_async_copy(src, dst, load_sem.at[i])
        c.start()
        loads.append(c)
    features = hidden_ref.shape[1]
    tall = token_ref.shape[0] // 2
    tok_a[z, rows(y * tall, tall), :] = token_ref[pl.ds(0, tall), :]
    tok_b[y, rows(z * tall, tall), :] = token_ref[pl.ds(tall, tall), :]
    greet(peers)

    def ring_sems(i):
        return (lambda way, k, h: ring_send.at[i, way, k, h]), (lambda way, k, h: ring_recv.at[i, way, k, h])

    at_y = lambda p: device(x, p, z, core)
    at_z = lambda p: device(x, y, p, core)
    cut = features // 2

    def wide_part(h):
        return pl.ds(0, cut) if h == 0 else pl.ds(cut, cut + GATES)

    a_y = Gather(NY, y, at_y, *ring_sems(0), lambda i, h: tok_a.at[z, rows(i * tall, tall), wide_part(h)])
    b_z = Gather(NZ, z, at_z, *ring_sems(1), lambda i, h: tok_b.at[y, rows(i * tall, tall), wide_part(h)])
    a_z = Gather(NZ, z, at_z, *ring_sems(2), lambda i, h: tok_a.at[i, pl.ds(h * 2 * tall, 2 * tall), :])
    b_y = Gather(NY, y, at_y, *ring_sems(3), lambda i, h: tok_b.at[i, pl.ds(h * 4 * tall, 4 * tall), :])

    own_expert = (y % 2) * 2 + core
    two_expert = (y % 2) * 2 + 1 - core
    tile = 256

    def experts(tok, block, out):
        size = tok.shape[1]

        @pl.loop(0, enter.shape[1] // tile)
        def _(n):
            columns = rows(n * tile, tile)
            act[pl.ds(0, size), columns] = jnp.dot(
                tok[block, :, pl.ds(0, features)], enter[:, columns], preferred_element_type=F32
            )

        sent = tok[block, :, pl.ds(features, GATES)].astype(F32)
        expert = lax.broadcasted_iota(jnp.int32, sent.shape, 1) % 4
        for s, e in ((0, own_expert), (1, two_expert)):
            weight = jnp.sum(jnp.where(expert == e, sent, 0.0), axis=-1, keepdims=True)
            g = act[pl.ds(0, size), pl.ds(2 * s * width, width)]
            u = act[pl.ds(0, size), pl.ds((2 * s + 1) * width, width)]
            inner[pl.ds(0, size), pl.ds(s * width, width)] = (g / (1.0 + jnp.exp(-g)) * u * weight).astype(BF16)

        @pl.loop(0, features // tile)
        def _(n):
            columns = rows(n * tile, tile)
            out[block, :, columns] = jnp.dot(
                inner[pl.ds(0, size), :], leave[:, columns], preferred_element_type=F32
            ).astype(BF16)

    def do_a(k):
        def body(i, carry):
            experts(tok_a, (z + k * (1 - 2 * i) + NZ) % NZ, sum_a)
            return carry

        def go():
            if k == 0:
                for c in loads:
                    c.wait()
            lax.fori_loop(0, 1 if k in (0, 4) else 2, body, 0)
        return go

    def do_b(k):
        def body(i, carry):
            experts(tok_b, (y + k * (1 - 2 * i) + NY) % NY, sum_b)
            return carry

        return lambda: lax.fori_loop(0, 1 if k in (0, 2) else 2, body, 0)

    gather_all(a_y, b_z, a_z, b_y, {
        "a0": do_a(0), "a1": do_a(1), "a2": do_a(2), "a3": do_a(3), "a4": do_a(4),
        "b0": do_b(0), "b1": do_b(1), "b2": do_b(2),
    })

    def narrow_part(h):
        return pl.ds(h * cut, cut)

    s_az = Scatter(NZ, z, at_z, *ring_sems(4), lambda i, h: sum_a.at[i, pl.ds(h * 2 * tall, 2 * tall), :],
                   lambda way, k, h: land_az.at[way, k, pl.ds(h * 2 * tall, 2 * tall), :])
    s_by = Scatter(NY, y, at_y, *ring_sems(5), lambda i, h: sum_b.at[i, pl.ds(h * 4 * tall, 4 * tall), :],
                   lambda way, k, h: land_by.at[way, k, pl.ds(h * 4 * tall, 4 * tall), :])
    s_ay = Scatter(NY, y, at_y, *ring_sems(6), lambda i, h: sum_a.at[z, rows(i * tall, tall), narrow_part(h)],
                   lambda way, k, h: land_ay.at[way, k, :, narrow_part(h)])
    s_bz = Scatter(NZ, z, at_z, *ring_sems(7), lambda i, h: sum_b.at[y, rows(i * tall, tall), narrow_part(h)],
                   lambda way, k, h: land_bz.at[way, k, :, narrow_part(h)])
    s_by.first()
    s_az.first()
    s_az.advance(1)
    s_by.advance(1)
    s_az.advance(2)
    s_az.advance(3)
    s_by.advance(2)
    s_bz.first()
    s_az.advance(4)
    s_ay.first()
    s_bz.advance(1)
    s_ay.advance(1)
    s_bz.advance(2)
    s_ay.advance(2)
    s_bz.advance(3)
    s_bz.advance(4)

    low, high = pl.ds(0, tall), pl.ds(tall, tall)
    mixed[x, low, :] = (hidden_ref[low, :] + sum_a[z, rows(y * tall, tall), :].astype(F32)).astype(BF16)
    mixed[x, high, :] = (hidden_ref[high, :] + sum_b[y, rows(z * tall, tall), :].astype(F32)).astype(BF16)
    lanes = []
    for dx in (1, 2, 3):
        c = pltpu.make_async_remote_copy(
            src_ref=mixed.at[x], dst_ref=mixed.at[x],
            send_sem=lane_send.at[dx], recv_sem=lane_recv.at[dx],
            device_id=device((x + dx) % NX, y, z, core), device_id_type=MESH,
        )
        c.start()
        lanes.append(c)
    few = 2 * tall
    out_ref[rows(x * few, few), :] = mixed[x]
    for dx in (1, 2, 3):
        source = (x + NX - dx) % NX
        land = mixed.at[source]
        pltpu.make_async_remote_copy(
            src_ref=land, dst_ref=land,
            send_sem=lane_send.at[dx], recv_sem=lane_recv.at[dx],
            device_id=device(source, y, z, core), device_id_type=MESH,
        ).wait_recv()
        out_ref[rows(source * few, few), :] = mixed[source]
    for ring in (a_y, b_z, a_z, b_y, s_az, s_by, s_ay, s_bz):
        ring.drain()
    for c in lanes:
        c.wait_send()


def local(
    context, residual, branch_out_proj, norm_gain, router, expert_ids, gate_proj, up_proj, down_proj
):
    token_count, features = residual.shape
    few = token_count // NX
    half = few // 2
    width = gate_proj.shape[2]
    tall, wide = branch_out_proj.shape[1] // 2, branch_out_proj.shape[2] // 2
    vmem, hbm = pl.BlockSpec(memory_space=pltpu.VMEM), pl.BlockSpec(memory_space=pl.ANY)
    dma = pltpu.SemaphoreType.DMA
    router_lanes = jnp.pad(jnp.concatenate([router] * 3, axis=1), ((0, 0), (0, GATES - 12)))
    gate, up, down = gate_proj[0], up_proj[0], down_proj[0]
    shaped = jax.ShapeDtypeStruct
    tokens, hidden, gate_two, up_two, down_two = pl.pallas_call(
        project_kernel,
        out_shape=(
            shaped((few, features + GATES), BF16), shaped((few, features), F32),
            shaped(gate.shape, BF16), shaped(up.shape, BF16), shaped(down.shape, BF16),
        ),
        in_specs=[vmem] * 6 + [hbm] * 3,
        out_specs=(vmem, vmem, hbm, hbm, hbm),
        scratch_shapes=[
            pltpu.VMEM((token_count, features), BF16),
            pltpu.VMEM((3, tall, wide), BF16),
            pltpu.VMEM((NZ, NY * tall, wide), BF16),
            pltpu.VMEM((2, token_count, wide), F32),
            pltpu.VMEM((2, token_count, wide), BF16),
            pltpu.VMEM((2 * NX, few, wide), BF16),
            dma((7,)), dma((7,)), dma((4, 2, 4, 2)), dma((4, 2, 4, 2)), dma((8,)), dma((8,)),
        ],
        compiler_params=pltpu.CompilerParams(
            collective_id=0, has_side_effects=True, vmem_limit_bytes=40 * 2**20
        ),
        name="merge_and_project",
    )(branch_out_proj[0], context, residual, norm_gain.reshape(1, features), router_lanes, expert_ids, gate, up, down)
    return pl.pallas_call(
        expert_kernel,
        out_shape=shaped((token_count, features), BF16),
        in_specs=[vmem] * 2 + [hbm] * 6,
        out_specs=vmem,
        scratch_shapes=[
            pltpu.VMEM((NZ, NY * half, features + GATES), BF16),
            pltpu.VMEM((NY, NZ * half, features + GATES), BF16),
            pltpu.VMEM((features, 4 * width), BF16),
            pltpu.VMEM((2 * width, features), BF16),
            pltpu.VMEM((NZ * half, 4 * width), F32),
            pltpu.VMEM((NZ * half, 2 * width), BF16),
            pltpu.VMEM((NZ, NY * half, features), BF16),
            pltpu.VMEM((NY, NZ * half, features), BF16),
            pltpu.VMEM((2, 4, NY * half, features), BF16),
            pltpu.VMEM((2, 2, NZ * half, features), BF16),
            pltpu.VMEM((2, 2, half, features), BF16),
            pltpu.VMEM((2, 4, half, features), BF16),
            pltpu.VMEM((NX, few, features), BF16),
            dma((6,)), dma((8, 2, 4, 2)), dma((8, 2, 4, 2)), dma((4,)), dma((4,)),
        ],
        compiler_params=pltpu.CompilerParams(
            collective_id=1, has_side_effects=True, vmem_limit_bytes=60 * 2**20
        ),
        name="experts",
    )(tokens, hidden, gate, up, down, gate_two, up_two, down_two)


def solution(mesh):
    placed = (
        P(("branch", "dp"), None),
        P(("branch", "dp"), None),
        P("branch", "dp", "mp"),
        P(),
        P(),
        P(("branch", "dp"), None),
        P("branch", None, "dp"),
        P("branch", None, "dp"),
        P("branch", "dp", None),
    )
    return jax.shard_map(
        local, mesh=mesh, in_specs=placed, out_specs=P(("branch", "dp"), None), check_vma=False
    )
```

time: 726 us -> 252 us (0.35)
  waiting for transfers between devices: 614 us -> 0 us
  Pallas kernels: 0 us -> 237 us
  matrix products: 38.6 us -> 0 us
  blocking collectives: 29.8 us -> 0 us
  between operations: 13.6 us -> 0.07 us
  other arithmetic: 9.21 us -> 0.93 us
    all_gather x4 -> x0, waiting for transfers between devices: 336 us -> none  [the longest x1 147 us: local(): shard_rows = lax.all_gather(arrived, 'dp', axis=0, tiled=True)]
    pallas_call x0 -> x2, Pallas kernels: none -> 237 us  [the longest x1 177 us: local(): pl.pallas_call(expert_kernel, out_shape=shaped((token_count, features), B...]
    reduce_scatter x1 -> x0, waiting for transfers between devices: 229 us -> none  [local(): lax.psum_scatter(block_terms.astype(jnp.bfloat16), 'dp', scatter_dimensio...]
    psum x1 -> x0, waiting for transfers between devices: 47.7 us -> none  [local(): lax.psum(own_block.astype(jnp.bfloat16), 'branch').astype(jnp.float32)]
    dot_general x6 -> x0, matrix products: 38.6 us -> none  [the longest x1 15.9 us: local(): jnp.dot(hidden_act, down_proj[0], preferred_element_type=jnp.float32)]
    all_to_all x2 -> x0, blocking collectives: 29.8 us -> none  [the longest x1 15 us: local(): lax.all_to_all(expert_out.reshape(branch_count, cap_lane, feature_count),...]
  transfers between devices with their start and end apart: 6 -> 0, of which waited for: 6 -> 0; matrix products, arithmetic and copies ran while one was open for 1% -> 0% of each run, Pallas kernels for 0% -> 0%
where the time goes in v1:
time: 252 us; the launch traced here: 251 us
  Pallas kernels  237 us (94%)
  local copies, waits for them, and re-layouts  13.3 us (5%)
    pallas_call x1, Pallas kernels, local(): pl.pallas_call(expert_kernel, out_shape=shaped((token_count, features), B...  177 us
    pallas_call x1, Pallas kernels, local(): pl.pallas_call(project_kernel, out_shape=(shaped((few, features + GATES),...  59.6 us
    unnamed x18, local copies, waits for them, and re-layouts  9.62 us

profile of v1, /device:TPU:8, one launch (start us, length us, event | category | flops | bytes accessed | tf_op | source)
XLA Modules:
  0.0 251.3 jit_solution(9143636782274017424)
XLA Ops:
  0.0 0.0 copy-start.5
  0.0 0.0 copy-start.4
  0.0 0.0 copy-start.3
  0.0 0.9 reshape.3.gain_ref
  0.9 0.8 copy.15.ids_ref
  1.7 0.9 pad_maximum_fusion
  2.6 1.4 copy.14
  4.0 1.4 pad.4.router_ref
  5.4 0.0 copy-done.5
  5.4 0.0 copy-done.4
  5.4 0.0 copy-done.3
  5.4 59.6 %merge_and_project.1 = (bf16[32,4224]{1,0:T(8,128)(2,1)S(1)}, f32[32,4096]{1,0:T(8,128)S(1)}, bf16[4096,384]{1,0:T(8,128)(2,1)S(1)}, bf16[4096,384]{1,0:T(8,128)(2,1)S(1)}, bf16[384,4096]{1,0:T(8,128)(2,1)S(1)}) custom-call(bf16[256,1024]{1,0:T(8,128)(2,1)S(1)} %bitcast.4, bf16[128,4096]{1,0:T(8,128)(2,1)S(1)} %copy-done.3, bf16[128,4096]{1,0:T(8,128)(2,1)S(1)} %copy-done.4, ...), custom_call_target="tpu_custom_call" | custom-call | tf_op jit(solution)/shard_map/merge_and_project/pallas_call | solution.py:463
  65.0 0.0 copy-start
  65.0 1.6 copy-done
  66.6 0.0 copy-start.1
  66.6 1.7 copy-done.1
  68.3 0.0 copy-start.2
  68.3 1.7 copy-done.2
  70.0 0.0 copy-start.6
  70.1 0.8 copy-done.6
  70.8 0.0 copy-start.7
  70.8 0.7 copy-done.7
  71.6 177.5 %experts.1 = bf16[128,4096]{1,0:T(8,128)(2,1)} custom-call(bf16[32,4224]{1,0:T(8,128)(2,1)} %copy-done.7, f32[32,4096]{1,0:T(8,128)} %copy-done.6, bf16[4096,384]{1,0:T(8,128)(2,1)} %bitcast.6, bf16[4096,384]{1,0:T(8,128)(2,1)} %bitcast.8, bf16[384,4096]{1,0:T(8,128)(2,1)} %bitcast.10, bf16[4096,384]{1,0:T(8,128)(2,1)} %copy-done, ...), custom_call_target="tpu_custom_call" | custom-call | tf_op jit(solution)/shard_map/experts/pallas_call | solution.py:485
  249.0 2.3 copy.17
Async XLA Ops:
  0.0 5.4 %copy-start.5 = (bf16[1,256,1024]{2,1,0:T(8,128)(2,1)S(1)}, bf16[1,256,1024]{2,1,0:T(8,128)(2,1)}, u32[]{:S(2)}) copy-start(bf16[1,256,1024]{2,1,0:T(8,128)(2,1)} %param.11) | copy-start | bytes 1572868
  0.0 5.4 %copy-start.4 = (bf16[128,4096]{1,0:T(8,128)(2,1)S(1)}, bf16[128,4096]{1,0:T(8,128)(2,1)}, u32[]{:S(2)}) copy-start(bf16[128,4096]{1,0:T(8,128)(2,1)} %residual_ref.1) | copy-start | bytes 3145732
  0.0 5.4 %copy-start.3 = (bf16[128,4096]{1,0:T(8,128)(2,1)S(1)}, bf16[128,4096]{1,0:T(8,128)(2,1)}, u32[]{:S(2)}) copy-start(bf16[128,4096]{1,0:T(8,128)(2,1)} %context_ref.1) | copy-start | bytes 3145732
  65.0 1.6 copy-start
  66.6 1.7 copy-start.1
  68.3 1.7 copy-start.2
  70.0 0.8 copy-start.6
  70.8 0.7 copy-start.7

commit v2 on v0

v2 whole, which is shorter than its diff:
```python
import jax
import jax.numpy as jnp
from jax import lax
from jax.experimental import pallas as pl
from jax.experimental.pallas import tpu as pltpu
from jax.sharding import PartitionSpec as P

NX, NY, NZ = 4, 4, 8
MESH = pl.DeviceIdType.MESH
F32, BF16 = jnp.float32, jnp.bfloat16
GATES = 128
FIRST, SECOND = 0, 1


def position():
    b, d, x = lax.axis_index("branch"), lax.axis_index("dp"), lax.axis_index("mp")
    return x, (d % 2) * 2 + b // 2, d // 2, b % 2


def device(x, y, z, core):
    return {"branch": (y % 2) * 2 + core, "dp": z * 2 + y // 2, "mp": x}


def rows(start, size):
    return pl.ds(pl.multiple_of(start, size), size)


class Ring:
    def __init__(self, n, me, at, send, recv):
        self.n, self.me, self.at, self.send_sem, self.recv_sem = n, me, at, send, recv
        self.sent = []

    def near(self, step):
        return (self.me + step + self.n) % self.n

    def copy(self, src, dst, k, h, way):
        return pltpu.make_async_remote_copy(
            src_ref=src,
            dst_ref=dst,
            send_sem=self.send_sem(way, k - 1, h),
            recv_sem=self.recv_sem(way, k - 1, h),
            device_id=self.at(self.near(1 if way == 0 else -1)),
            device_id_type=MESH,
        )

    def launch(self, src, dst, k, h, way):
        c = self.copy(src, dst, k, h, way)
        c.start()
        self.sent.append(c)

    def drain(self):
        for c in self.sent:
            c.wait_send()


class Gather(Ring):
    def __init__(self, n, me, at, send, recv, block, sliding=False):
        super().__init__(n, me, at, send, recv)
        self.block, self.sliding, self.seen = block, sliding, set()

    def lanes(self, k, turn):
        if turn == SECOND and k == self.n // 2:
            return []
        return [(way if turn == FIRST else 1 - way, way) for way in (0, 1)]

    def hop(self, k, h, way):
        if k > 1:
            self.arrive(k - 1, h, way)
        sign = -1 if way == 0 else 1
        src = self.block(sign * (k - 1), h)
        self.launch(src, self.block(sign * k, h) if self.sliding else src, k, h, way)

    def start(self, k, turn=None):
        for t in (FIRST, SECOND) if turn is None else (turn,):
            for h, way in self.lanes(k, t):
                self.hop(k, h, way)

    def arrive(self, k, h, way):
        if (k, h, way) not in self.seen:
            self.seen.add((k, h, way))
            part = self.block(-k if way == 0 else k, h)
            self.copy(part, part, k, h, way).wait_recv()

    def arrived(self, k):
        for t in (FIRST, SECOND):
            for h, way in self.lanes(k, t):
                self.arrive(k, h, way)


class Scatter(Ring):
    def __init__(self, n, me, at, send, recv, block, landing):
        super().__init__(n, me, at, send, recv)
        self.block, self.landing = block, landing

    def put(self, k, h, way):
        far = self.n // 2 - k + 1
        self.launch(self.block(far if way == 0 else -far, h), self.landing(way, k - 1, h), k, h, way)

    def first(self):
        for way in (0, 1):
            self.put(1, way, way)
        for way in (0, 1):
            self.put(2, 1 - way, way)

    def advance(self, k, turn=None):
        for t in (FIRST, SECOND) if turn is None else (turn,):
            if k == 1 and t == FIRST:
                continue
            for way in (0, 1):
                h = 1 - way if t == FIRST else way
                arrived = self.landing(way, k - 1, h)
                self.copy(arrived, arrived, k, h, way).wait_recv()
                left = self.n // 2 - k
                mine = self.block(left if way == 0 else -left, h)
                mine[...] = (mine[...].astype(F32) + arrived[...].astype(F32)).astype(BF16)
                if left:
                    self.put(k + 1, h, way)


def greet(peers):
    barrier = pltpu.get_barrier_semaphore()
    for peer in peers:
        pl.semaphore_signal(barrier, inc=1, device_id=peer, device_id_type=MESH)
    pl.semaphore_wait(barrier, len(peers))


A_ROWS = {0: 0, -1: 192, 1: 256, -2: 320, 2: 384, -3: 704, 3: 768, 4: 832, -4: 832}
B_ROWS = {0: 64, -1: 448, 1: 576, 2: 896, -2: 896}


def layer_kernel(
    block_ref, context_ref, residual_ref, gain_ref, router_ref, ids_ref, gate_ref, up_ref, down_ref,
    out_ref,
    context_all, pieces, merged, total, part, parts, hidden_ref,
    tok, enter, leave, act, inner, sums, land_az, land_by, land_ay, land_bz, mixed,
    load_sem, pair_send, pair_recv, ring_send, ring_recv, lane_send, lane_recv,
):
    x, y, z, core = position()
    other = 1 - core
    half = y % 2
    base = y - half
    mate = base + 1 - half
    width = gate_ref.shape[1]
    tokens, features = context_ref.shape
    loads = []
    for i, (src, dst) in enumerate((
        (context_ref, context_all.at[pl.ds(0, tokens), :]),
        (gate_ref, enter.at[:, pl.ds(0, width)]),
        (up_ref, enter.at[:, pl.ds(width, width)]),
        (down_ref, leave.at[pl.ds(0, width), :]),
    )):
        c = pltpu.make_async_copy(src, dst, load_sem.at[i])
        c.start()
        loads.append(c)
    peers = [device(x, y, z, other), device(x, mate, z, core), device(x, mate, z, other)]
    far_side = (y + 1 + 2 * (1 - half)) % NY
    peers += [device(x, far_side, z, core), device(x, y, (z + 1) % NZ, core), device(x, y, (z + 7) % NZ, core)]
    for dx in (1, 2, 3):
        for c in (core, other):
            peers.append(device((x + dx) % NX, y, z, c))
    greet(peers)

    def pair_copy(i, src, dst, to):
        return pltpu.make_async_remote_copy(
            src_ref=src, dst_ref=dst, send_sem=pair_send.at[i], recv_sem=pair_recv.at[i],
            device_id=to, device_id_type=MESH,
        )

    tall, wide = block_ref.shape[0] // 2, block_ref.shape[1] // 2
    sibling = device(x, y, z, other)
    pending = []
    for i, (dy, dc) in enumerate(((0, 1), (1, 0), (1, 1))):
        to_half = half if dy == 0 else 1 - half
        to_core = core if dc == 0 else other
        pending.append(pair_copy(
            i, block_ref.at[rows(to_half * tall, tall), rows(to_core * wide, wide)], pieces.at[i],
            device(x, base + to_half, z, to_core),
        ))
    pending.append(pair_copy(3, context_ref, context_all.at[pl.ds(tokens, tokens), :], sibling))
    pending.append(pair_copy(4, gate_ref, enter.at[:, pl.ds(2 * width, width)], sibling))
    pending.append(pair_copy(5, up_ref, enter.at[:, pl.ds(3 * width, width)], sibling))
    pending.append(pair_copy(6, down_ref, leave.at[pl.ds(width, width), :], sibling))
    for c in pending:
        c.start()
    for c in pending[:3]:
        c.wait_recv()
    own = block_ref[rows(half * tall, tall), rows(core * wide, wide)].astype(F32)
    own = own + pieces[0].astype(F32) + pieces[1].astype(F32) + pieces[2].astype(F32)
    merged[z, rows(y * tall, tall), :] = (own * 0.25).astype(BF16)

    quarter = wide // 2

    def ring_sems(i):
        return (lambda way, k, h: ring_send.at[i, way, k, h]), (lambda way, k, h: ring_recv.at[i, way, k, h])

    at_y = lambda p: device(x, p, z, core)
    at_z = lambda p: device(x, y, p, core)
    near_y = lambda r: (y + r + NY) % NY
    near_z = lambda r: (z + r + NZ) % NZ
    piece = tall // 2
    a_y = Gather(NY, y, at_y, *ring_sems(0), lambda r, h: merged.at[
        z, rows(near_y(r) * tall + h * piece, piece), pl.ds(0, quarter)])
    b_z = Gather(NZ, z, at_z, *ring_sems(1), lambda r, h: merged.at[
        near_z(r), rows(y * tall + h * piece, piece), pl.ds(quarter, quarter)])
    a_z = Gather(NZ, z, at_z, *ring_sems(2), lambda r, h: merged.at[
        near_z(r), pl.ds(h * 2 * tall, 2 * tall), pl.ds(0, quarter)])
    b_y = Gather(NY, y, at_y, *ring_sems(3), lambda r, h: merged.at[
        pl.ds(h * 4, 4), rows(near_y(r) * tall, tall), pl.ds(quarter, quarter)])
    rings = [a_y, b_z, a_z, b_y]

    left, right = pl.ds(0, quarter), pl.ds(quarter, quarter)

    def project_a(*distances):
        for r in distances:
            i = near_z(r)
            term = jnp.dot(
                context_all[:, rows(i * 4 * tall, 4 * tall)], merged[i, :, left], preferred_element_type=F32
            )
            total[:, left] = term if r == 0 else total[:, left] + term

    def project_b(*distances):
        for r in distances:
            i = near_y(r)
            term = None
            for k in range(NZ):
                one = jnp.dot(
                    context_all[:, rows(i * tall + k * 4 * tall, tall)], merged[k, rows(i * tall, tall), right],
                    preferred_element_type=F32,
                )
                term = one if term is None else term + one
            total[:, right] = term if r == 0 else total[:, right] + term

    short_phase(a_y, b_z, a_z, b_y)
    loads[0].wait()
    pending[3].wait_recv()
    project_a(0)
    a_z.start(2, FIRST)
    project_b(0)
    a_z.start(2, SECOND)
    project_a(-1, 1)
    b_y.start(2)
    a_z.start(3, FIRST)
    a_z.start(3, SECOND)
    project_a(-2, 2)
    b_y.arrived(1)
    a_z.start(4)
    project_b(-1, 1)
    a_z.arrived(3)
    project_a(-3, 3)
    b_y.arrived(2)
    project_b(2)
    a_z.arrived(4)
    project_a(4)

    part[...] = total[...].astype(BF16)
    few = tokens // NX
    parts[x * 2 + core] = part[rows(x * few, few), :]
    lanes = []
    for dx in (2, 1, 3, 0):
        for dc in range(2):
            if dx or dc:
                to_x = (x + dx) % NX
                c = pltpu.make_async_remote_copy(
                    src_ref=part.at[rows(to_x * few + dc * tokens, few), :],
                    dst_ref=parts.at[x * 2 + core],
                    send_sem=lane_send.at[dx * 2 + dc], recv_sem=lane_recv.at[dx * 2 + dc],
                    device_id=device(to_x, y, z, core if dc == 0 else other), device_id_type=MESH,
                )
                c.start()
                lanes.append((dx, dc, c))
    for dx, dc, c in lanes:
        land = parts.at[(x + NX - dx) % NX * 2 + (core if dc == 0 else other)]
        pltpu.make_async_remote_copy(
            src_ref=land, dst_ref=land,
            send_sem=lane_send.at[dx * 2 + dc], recv_sem=lane_recv.at[dx * 2 + dc],
            device_id=sibling, device_id_type=MESH,
        ).wait_recv()
    here = rows(x * few, few)
    squares = jnp.zeros((few, 1), F32)
    for j in range(2 * NX):
        columns = pl.ds(j * wide, wide)
        hidden = residual_ref[here, columns].astype(F32) + parts[j].astype(F32)
        hidden_ref[:, columns] = hidden
        squares = squares + jnp.sum(hidden * hidden, axis=-1, keepdims=True)
    inv_rms = lax.rsqrt(squares / features + 1e-05)
    short = few // 2
    slot_a = rows(A_ROWS[0] + y * short, short)
    slot_b = rows(B_ROWS[0] + z * short, short)
    logits = jnp.zeros((few, 4), F32)
    for j in range(2 * NX):
        columns = pl.ds(j * wide, wide)
        normed = (hidden_ref[:, columns] * inv_rms * gain_ref[:, columns].astype(F32)).astype(BF16)
        tok[slot_a, columns] = normed[:short]
        tok[slot_b, columns] = normed[short:]
        logits = logits + lax.dot_general(
            normed, router_ref[:, columns], (((1,), (1,)), ((), ())), preferred_element_type=F32
        )
    lane = lax.broadcasted_iota(jnp.int32, (few, GATES), 1)
    row = lax.broadcasted_iota(jnp.int32, (few, GATES), 0)
    expert = lane % 4
    scores = 1.0 / (1.0 + jnp.exp(-logits))
    score_lanes = jnp.zeros((few, GATES), F32)
    for e in range(4):
        score_lanes = jnp.where(expert == e, scores[:, e:e + 1], score_lanes)
    ids = ids_ref[...].astype(F32)
    mine = lane == row + x * few
    first, second = (
        jnp.sum(jnp.where(mine, ids[k:k + 1, :], 0.0), axis=-1, keepdims=True) == expert.astype(F32) for k in (0, 1)
    )
    once = lane < 4
    picked_first = jnp.sum(jnp.where(first & once, score_lanes, 0.0), axis=-1, keepdims=True)
    picked_second = jnp.sum(jnp.where(second & once, score_lanes, 0.0), axis=-1, keepdims=True)
    weight = jnp.where(first, picked_first, jnp.where(second, picked_second, 0.0))
    weight = weight / (picked_first + picked_second)
    high = weight.astype(BF16).astype(F32)
    mid = (weight - high).astype(BF16).astype(F32)
    low = weight - high - mid
    sent = jnp.where(lane < 4, high, jnp.where(lane < 8, mid, jnp.where(lane < 12, low, 0.0))).astype(BF16)
    tok[slot_a, pl.ds(features, GATES)] = sent[:short]
    tok[slot_b, pl.ds(features, GATES)] = sent[short:]

    cut = features // 2

    def token_part(h):
        return pl.ds(0, cut) if h == 0 else pl.ds(cut, cut + GATES)

    def sum_part(h):
        return pl.ds(h * cut, cut)

    in_a = lambda p: rows(A_ROWS[0] + p * short, short)
    in_b = lambda p: rows(B_ROWS[0] + p * short, short)
    part_a = lambda r, h: pl.ds(A_ROWS[r] + h * 2 * short, 2 * short)
    part_b = lambda r, h: pl.ds(B_ROWS[r] + h * 4 * short, 4 * short)
    a_y = Gather(NY, y, at_y, *ring_sems(4), lambda r, h: tok.at[in_a(near_y(r)), token_part(h)])
    b_z = Gather(NZ, z, at_z, *ring_sems(5), lambda r, h: tok.at[in_b(near_z(r)), token_part(h)])
    a_z = Gather(NZ, z, at_z, *ring_sems(6), lambda r, h: tok.at[part_a(r, h), :], True)
    b_y = Gather(NY, y, at_y, *ring_sems(7), lambda r, h: tok.at[part_b(r, h), :], True)
    s_az = Scatter(NZ, z, at_z, *ring_sems(8), lambda r, h: sums.at[part_a(r, h), :],
                   lambda way, k, h: land_az.at[way, k, pl.ds(h * 2 * short, 2 * short), :])
    s_by = Scatter(NY, y, at_y, *ring_sems(9), lambda r, h: sums.at[part_b(r, h), :],
                   lambda way, k, h: land_by.at[way, k, pl.ds(h * 4 * short, 4 * short), :])
    s_ay = Scatter(NY, y, at_y, *ring_sems(10), lambda r, h: sums.at[in_a(near_y(r)), sum_part(h)],
                   lambda way, k, h: land_ay.at[way, k, :, sum_part(h)])
    s_bz = Scatter(NZ, z, at_z, *ring_sems(11), lambda r, h: sums.at[in_b(near_z(r)), sum_part(h)],
                   lambda way, k, h: land_bz.at[way, k, :, sum_part(h)])
    rings += [a_y, b_z, a_z, b_y, s_az, s_by, s_ay, s_bz]

    own_expert = half * 2 + core
    two_expert = half * 2 + other

    def expand(start, size):
        span, top = pl.ds(start, size), pl.ds(0, size)
        tile = 2 * width

        @pl.loop(0, 2)
        def _(n):
            columns = rows(n * tile, tile)
            act[top, columns] = jnp.dot(
                tok[span, pl.ds(0, features)], enter[:, columns], preferred_element_type=F32
            )

        gates = tok[span, pl.ds(features, GATES)].astype(F32)
        names = lax.broadcasted_iota(jnp.int32, gates.shape, 1) % 4
        for s, e in ((0, own_expert), (1, two_expert)):
            scale = jnp.sum(jnp.where(names == e, gates, 0.0), axis=-1, keepdims=True)
            g = act[top, pl.ds(2 * s * width, width)]
            u = act[top, pl.ds((2 * s + 1) * width, width)]
            inner[span, pl.ds(s * width, width)] = (g / (1.0 + jnp.exp(-g)) * u * scale).astype(BF16)

    def contract(start, size):
        span = pl.ds(start, size)
        tile = features // 2

        @pl.loop(0, 2)
        def _(n):
            columns = rows(n * tile, tile)
            sums[span, columns] = jnp.dot(
                inner[span, :], leave[:, columns], preferred_element_type=F32
            ).astype(BF16)

    short_phase(a_y, b_z, a_z, b_y)
    for c in loads[1:]:
        c.wait()
    for c in pending[4:]:
        c.wait_recv()
    expand(0, 192)
    a_z.start(2, FIRST)
    a_z.start(2, SECOND)
    expand(192, 128)
    b_y.start(2)
    a_z.start(3, FIRST)
    a_z.start(3, SECOND)
    expand(320, 128)
    b_y.arrived(1)
    a_z.start(4)
    expand(448, 256)
    contract(448, 256)
    a_z.arrived(3)
    expand(704, 128)
    contract(704, 128)
    b_y.arrived(2)
    expand(896, 128)
    contract(896, 128)
    s_by.first()
    a_z.arrived(4)
    expand(832, 64)
    contract(832, 64)
    s_az.first()
    contract(192, 256)
    contract(0, 192)
    s_az.advance(1)
    s_az.advance(2, FIRST)
    s_by.advance(1)
    s_az.advance(2, SECOND)
    s_az.advance(3, FIRST)
    s_by.advance(2, FIRST)
    s_az.advance(3, SECOND)
    s_az.advance(4, FIRST)
    s_by.advance(2, SECOND)
    s_bz.first()
    s_bz.advance(1)
    s_az.advance(4, SECOND)
    s_ay.first()
    s_bz.advance(2)
    s_ay.advance(1)
    s_bz.advance(3)
    s_ay.advance(2)

    c_x = Gather(NX, x, lambda p: device(p, y, z, core), *ring_sems(12), lambda r, h: mixed.at[
        (x + r + NX) % NX, pl.ds(h * short, short), :])
    rings.append(c_x)
    low, high = pl.ds(0, short), pl.ds(short, short)
    mixed[x, low, :] = (hidden_ref[low, :] + sums[slot_a, :].astype(F32)).astype(BF16)
    c_x.hop(1, 0, 0)
    c_x.hop(1, 0, 1)
    s_bz.advance(4)
    mixed[x, high, :] = (hidden_ref[high, :] + sums[slot_b, :].astype(F32)).astype(BF16)
    c_x.hop(1, 1, 1)
    c_x.hop(1, 1, 0)
    out_ref[here, :] = mixed[x]
    c_x.start(2)
    c_x.arrived(1)
    for r in (-1, 1):
        near = (x + r + NX) % NX
        out_ref[rows(near * few, few), :] = mixed[near]
    c_x.arrived(2)
    near = (x + 2) % NX
    out_ref[rows(near * few, few), :] = mixed[near]
    for c in pending:
        c.wait_send()
    for ring in rings:
        ring.drain()
    for _, _, c in lanes:
        c.wait_send()


def short_phase(a_y, b_z, a_z, b_y):
    a_y.start(1)
    b_z.start(1)
    a_y.start(2)
    b_z.start(2)
    a_y.arrived(1)
    a_y.arrived(2)
    a_z.start(1)
    b_z.start(3)
    b_z.start(4)
    for k in (1, 2, 3, 4):
        b_z.arrived(k)
    b_y.start(1)


def local(
    context, residual, branch_out_proj, norm_gain, router, expert_ids, gate_proj, up_proj, down_proj
):
    token_count, features = residual.shape
    few = token_count // NX
    half = few // 2
    width = gate_proj.shape[2]
    tall, wide = branch_out_proj.shape[1] // 2, branch_out_proj.shape[2] // 2
    vmem, hbm = pl.BlockSpec(memory_space=pltpu.VMEM), pl.BlockSpec(memory_space=pl.ANY)
    dma = pltpu.SemaphoreType.DMA
    plane = NY * NZ * few
    return pl.pallas_call(
        layer_kernel,
        out_shape=jax.ShapeDtypeStruct((token_count, features), BF16),
        in_specs=[vmem, hbm] + [vmem] * 4 + [hbm] * 3,
        out_specs=vmem,
        scratch_shapes=[
            pltpu.VMEM((2 * token_count, features), BF16),
            pltpu.VMEM((3, tall, wide), BF16),
            pltpu.VMEM((NZ, NY * tall, wide), BF16),
            pltpu.VMEM((2 * token_count, wide), F32),
            pltpu.VMEM((2 * token_count, wide), BF16),
            pltpu.VMEM((2 * NX, few, wide), BF16),
            pltpu.VMEM((few, features), F32),
            pltpu.VMEM((plane, features + GATES), BF16),
            pltpu.VMEM((features, 4 * width), BF16),
            pltpu.VMEM((2 * width, features), BF16),
            pltpu.VMEM((256, 4 * width), F32),
            pltpu.VMEM((plane, 2 * width), BF16),
            pltpu.VMEM((plane, features), BF16),
            pltpu.VMEM((2, 4, NY * half, features), BF16),
            pltpu.VMEM((2, 2, NZ * half, features), BF16),
            pltpu.VMEM((2, 2, half, features), BF16),
            pltpu.VMEM((2, 4, half, features), BF16),
            pltpu.VMEM((NX, few, features), BF16),
            dma((4,)), dma((7,)), dma((7,)), dma((13, 2, 4, 2)), dma((13, 2, 4, 2)), dma((8,)), dma((8,)),
        ],
        compiler_params=pltpu.CompilerParams(
            collective_id=0, has_side_effects=True, vmem_limit_bytes=62 * 2**20
        ),
        name="layer",
    )(
        branch_out_proj[0], context, residual, norm_gain.reshape(1, features), router.T, expert_ids.T,
        gate_proj[0], up_proj[0], down_proj[0],
    )


def solution(mesh):
    placed = (
        P(("branch", "dp"), None),
        P(("branch", "dp"), None),
        P("branch", "dp", "mp"),
        P(),
        P(),
        P(("branch", "dp"), None),
        P("branch", None, "dp"),
        P("branch", None, "dp"),
        P("branch", "dp", None),
    )
    return jax.shard_map(
        local, mesh=mesh, in_specs=placed, out_specs=P(("branch", "dp"), None), check_vma=False
    )
```

time: 726 us -> 198 us (0.27)
  waiting for transfers between devices: 614 us -> 0 us
  Pallas kernels: 0 us -> 194 us
  matrix products: 38.6 us -> 0 us
  blocking collectives: 29.8 us -> 0 us
  local copies, waits for them, and re-layouts: 19 us -> 3.6 us
  between operations: 13.6 us -> 0.01 us
  other arithmetic: 9.21 us -> 0 us
    all_gather x4 -> x0, waiting for transfers between devices: 336 us -> none  [the longest x1 147 us: local(): shard_rows = lax.all_gather(arrived, 'dp', axis=0, tiled=True)]
    reduce_scatter x1 -> x0, waiting for transfers between devices: 229 us -> none  [local(): lax.psum_scatter(block_terms.astype(jnp.bfloat16), 'dp', scatter_dimensio...]
    pallas_call x0 -> x1, Pallas kernels: none -> 194 us  [local(): pl.pallas_call(layer_kernel, out_shape=jax.ShapeDtypeStruct((token_count,...]
    psum x1 -> x0, waiting for transfers between devices: 47.7 us -> none  [local(): lax.psum(own_block.astype(jnp.bfloat16), 'branch').astype(jnp.float32)]
    dot_general x6 -> x0, matrix products: 38.6 us -> none  [the longest x1 15.9 us: local(): jnp.dot(hidden_act, down_proj[0], preferred_element_type=jnp.float32)]
    all_to_all x2 -> x0, blocking collectives: 29.8 us -> none  [the longest x1 15 us: local(): lax.all_to_all(expert_out.reshape(branch_count, cap_lane, feature_count),...]
  transfers between devices with their start and end apart: 6 -> 0, of which waited for: 6 -> 0; matrix products, arithmetic and copies ran while one was open for 1% -> 0% of each run, Pallas kernels for 0% -> 0%
where the time goes in v2:
time: 198 us
  Pallas kernels  194 us (98%)
  local copies, waits for them, and re-layouts  3.6 us (2%)
    pallas_call x1, Pallas kernels, local(): pl.pallas_call(layer_kernel, out_shape=jax.ShapeDtypeStruct((token_count,...  194 us

profile of v2, /device:TPU:8, one launch (start us, length us, event | category | flops | bytes accessed | tf_op | source)
XLA Modules:
  0.0 197.5 jit_solution(14972250054497428561)
XLA Ops:
  0.0 1.3 reshape.3.gain_ref
  1.3 193.9 %layer.1 = bf16[128,4096]{1,0:T(8,128)(2,1)} custom-call(bf16[256,1024]{1,0:T(8,128)(2,1)} %bitcast.9, bf16[128,4096]{1,0:T(8,128)(2,1)} %context_ref.1, bf16[128,4096]{1,0:T(8,128)(2,1)} %residual_ref.1, bf16[1,4096]{1,0:T(2,128)(2,1)} %reshape.3.gain_ref, bf16[4,4096]{1,0:T(4,128)(2,1)} %bitcast.10, s32[2,128]{1,0:T(2,128)} %bitcast.11, ...), custom_call_target="tpu_custom_call" | custom-call | tf_op jit(solution)/shard_map/layer/pallas_call | solution.py:483
  195.2 2.3 %copy.11 = bf16[128,4096]{1,0:T(8,128)(2,1)} copy(bf16[128,4096]{1,0:T(8,128)(2,1)} %layer.1) | data formatting | bytes 2097152

commit v3 on v2

--- a/solution.py
+++ b/solution.py
@@ -43,14 +43,13 @@
             device_id_type=MESH,
         )
 
-    def launch(self, src, dst, k, h, way):
-        c = self.copy(src, dst, k, h, way)
-        c.start()
-        self.sent.append(c)
+    def launch(self, k, h, way):
+        self.copy(*self.ends(k, h, way), k, h, way).start()
+        self.sent.append((k, h, way))
 
     def drain(self):
-        for c in self.sent:
-            c.wait_send()
+        for k, h, way in self.sent:
+            self.copy(*self.ends(k, h, way), k, h, way).wait_send()
 
 
 class Gather(Ring):
@@ -66,9 +65,12 @@
     def hop(self, k, h, way):
         if k > 1:
             self.arrive(k - 1, h, way)
+        self.launch(k, h, way)
+
+    def ends(self, k, h, way):
         sign = -1 if way == 0 else 1
         src = self.block(sign * (k - 1), h)
-        self.launch(src, self.block(sign * k, h) if self.sliding else src, k, h, way)
+        return src, self.block(sign * k, h) if self.sliding else src
 
     def start(self, k, turn=None):
         for t in (FIRST, SECOND) if turn is None else (turn,):
@@ -92,15 +94,20 @@
         super().__init__(n, me, at, send, recv)
         self.block, self.landing = block, landing
 
+    def ends(self, k, h, way):
+        far = self.n // 2 - k + 1
+        return self.block(far if way == 0 else -far, h), self.landing(way, k - 1, h)
+
     def put(self, k, h, way):
-        far = self.n // 2 - k + 1
-        self.launch(self.block(far if way == 0 else -far, h), self.landing(way, k - 1, h), k, h, way)
-
-    def first(self):
+        self.launch(k, h, way)
+
+    def near_terms(self):
+        for way in (0, 1):
+            self.put(2, 1 - way, way)
+
+    def far_terms(self):
         for way in (0, 1):
             self.put(1, way, way)
-        for way in (0, 1):
-            self.put(2, 1 - way, way)
 
     def advance(self, k, turn=None):
         for t in (FIRST, SECOND) if turn is None else (turn,):
@@ -112,7 +119,7 @@
                 self.copy(arrived, arrived, k, h, way).wait_recv()
                 left = self.n // 2 - k
                 mine = self.block(left if way == 0 else -left, h)
-                mine[...] = (mine[...].astype(F32) + arrived[...].astype(F32)).astype(BF16)
+                add_into(mine, arrived)
                 if left:
                     self.put(k + 1, h, way)
 
@@ -124,15 +131,15 @@
     pl.semaphore_wait(barrier, len(peers))
 
 
-A_ROWS = {0: 0, -1: 192, 1: 256, -2: 320, 2: 384, -3: 704, 3: 768, 4: 832, -4: 832}
-B_ROWS = {0: 64, -1: 448, 1: 576, 2: 896, -2: 896}
+A_ROWS = {0: 0, 4: 64, -4: 64, -1: 256, 1: 320, -2: 384, 2: 448, -3: 768, 3: 832}
+B_ROWS = {0: 128, -1: 512, 1: 640, 2: 896, -2: 896}
 
 
 def layer_kernel(
     block_ref, context_ref, residual_ref, gain_ref, router_ref, ids_ref, gate_ref, up_ref, down_ref,
     out_ref,
     context_all, pieces, merged, total, part, parts, hidden_ref,
-    tok, enter, leave, act, inner, sums, land_az, land_by, land_ay, land_bz, mixed,
+    tok, enter, leave, act, inner, sums, land_az, land_by, land_ay, land_bz,
     load_sem, pair_send, pair_recv, ring_send, ring_recv, lane_send, lane_recv,
 ):
     x, y, z, core = position()
@@ -180,10 +187,12 @@
     pending.append(pair_copy(4, gate_ref, enter.at[:, pl.ds(2 * width, width)], sibling))
     pending.append(pair_copy(5, up_ref, enter.at[:, pl.ds(3 * width, width)], sibling))
     pending.append(pair_copy(6, down_ref, leave.at[pl.ds(width, width), :], sibling))
-    for c in pending:
+    for c in pending[:4]:
         c.start()
     for c in pending[:3]:
         c.wait_recv()
+    for c in pending[4:]:
+        c.start()
     own = block_ref[rows(half * tall, tall), rows(core * wide, wide)].astype(F32)
     own = own + pieces[0].astype(F32) + pieces[1].astype(F32) + pieces[2].astype(F32)
     merged[z, rows(y * tall, tall), :] = (own * 0.25).astype(BF16)
@@ -210,47 +219,44 @@
 
     left, right = pl.ds(0, quarter), pl.ds(quarter, quarter)
 
-    def project_a(*distances):
-        for r in distances:
-            i = near_z(r)
-            term = jnp.dot(
-                context_all[:, rows(i * 4 * tall, 4 * tall)], merged[i, :, left], preferred_element_type=F32
-            )
-            total[:, left] = term if r == 0 else total[:, left] + term
-
-    def project_b(*distances):
-        for r in distances:
-            i = near_y(r)
-            term = None
-            for k in range(NZ):
-                one = jnp.dot(
-                    context_all[:, rows(i * tall + k * 4 * tall, tall)], merged[k, rows(i * tall, tall), right],
-                    preferred_element_type=F32,
-                )
-                term = one if term is None else term + one
-            total[:, right] = term if r == 0 else total[:, right] + term
-
-    short_phase(a_y, b_z, a_z, b_y)
-    loads[0].wait()
-    pending[3].wait_recv()
-    project_a(0)
-    a_z.start(2, FIRST)
-    project_b(0)
-    a_z.start(2, SECOND)
-    project_a(-1, 1)
-    b_y.start(2)
-    a_z.start(3, FIRST)
-    a_z.start(3, SECOND)
-    project_a(-2, 2)
-    b_y.arrived(1)
-    a_z.start(4)
-    project_b(-1, 1)
-    a_z.arrived(3)
-    project_a(-3, 3)
-    b_y.arrived(2)
-    project_b(2)
-    a_z.arrived(4)
-    project_a(4)
+    def project_a(r):
+        i = near_z(r)
+        total[:, left] += jnp.dot(
+            context_all[:, rows(i * 4 * tall, 4 * tall)], merged[i, :, left], preferred_element_type=F32
+        )
+
+    def project_b(r):
+        i = near_y(r)
+        terms = [
+            jnp.dot(
+                context_all[:, rows(i * tall + k * 4 * tall, tall)], merged[k, rows(i * tall, tall), right],
+                preferred_element_type=F32,
+            ) for k in range(NZ)
+        ]
+        total[:, right] += sum(terms[1:], terms[0])
+
+    total[...] = jnp.zeros_like(total)
+
+    def ready_context():
+        loads[0].wait()
+        pending[3].wait_recv()
+
+    order = interleave(gather_events(a_y, b_z, a_z, b_y, 1.8, 7.0, 2.7), [
+        ("a0", {"ay"}, 0.5, ("a", 0), None),
+        ("b0", {"bz"}, 0.8, ("b", 0), None),
+        ("a1m", {"az1"}, 0.5, ("a", -1), None),
+        ("a1p", {"az1"}, 0.5, ("a", 1), None),
+        ("a2m", {"az2"}, 0.5, ("a", -2), None),
+        ("a2p", {"az2"}, 0.5, ("a", 2), None),
+        ("b1m", {"by1"}, 0.8, ("b", -1), None),
+        ("b1p", {"by1"}, 0.8, ("b", 1), None),
+        ("a3m", {"az3"}, 0.5, ("a", -3), None),
+        ("a3p", {"az3"}, 0.5, ("a", 3), None),
+        ("b2", {"by2"}, 0.8, ("b", 2), None),
+        ("a4", {"az4"}, 0.5, ("a", 4), None),
+    ])
+    first_step = next(i for i, item in enumerate(order) if not callable(item))
+    run_in_order(order[:first_step] + [ready_context] + order[first_step:], {"a": project_a, "b": project_b})
 
     part[...] = total[...].astype(BF16)
     few = tokens // NX
@@ -324,8 +330,11 @@
     def token_part(h):
         return pl.ds(0, cut) if h == 0 else pl.ds(cut, cut + GATES)
 
-    def sum_part(h):
-        return pl.ds(h * cut, cut)
+    def columns_of(c):
+        return pl.ds(c * cut, cut)
+
+    def sum_part(c, h):
+        return pl.ds(c * cut + h * (cut // 2), cut // 2)
 
     in_a = lambda p: rows(A_ROWS[0] + p * short, short)
     in_b = lambda p: rows(B_ROWS[0] + p * short, short)
@@ -335,117 +344,128 @@
     b_z = Gather(NZ, z, at_z, *ring_sems(5), lambda r, h: tok.at[in_b(near_z(r)), token_part(h)])
     a_z = Gather(NZ, z, at_z, *ring_sems(6), lambda r, h: tok.at[part_a(r, h), :], True)
     b_y = Gather(NY, y, at_y, *ring_sems(7), lambda r, h: tok.at[part_b(r, h), :], True)
-    s_az = Scatter(NZ, z, at_z, *ring_sems(8), lambda r, h: sums.at[part_a(r, h), :],
-                   lambda way, k, h: land_az.at[way, k, pl.ds(h * 2 * short, 2 * short), :])
-    s_by = Scatter(NY, y, at_y, *ring_sems(9), lambda r, h: sums.at[part_b(r, h), :],
-                   lambda way, k, h: land_by.at[way, k, pl.ds(h * 4 * short, 4 * short), :])
-    s_ay = Scatter(NY, y, at_y, *ring_sems(10), lambda r, h: sums.at[in_a(near_y(r)), sum_part(h)],
-                   lambda way, k, h: land_ay.at[way, k, :, sum_part(h)])
-    s_bz = Scatter(NZ, z, at_z, *ring_sems(11), lambda r, h: sums.at[in_b(near_z(r)), sum_part(h)],
-                   lambda way, k, h: land_bz.at[way, k, :, sum_part(h)])
-    rings += [a_y, b_z, a_z, b_y, s_az, s_by, s_ay, s_bz]
+    s_az, s_by, s_ay, s_bz, s_x = [], [], [], [], []
+    for c in range(2):
+        s_az.append(Scatter(
+            NZ, z, at_z, *ring_sems(8 + 5 * c), lambda r, h, c=c: sums.at[part_a(r, h), columns_of(c)],
+            lambda way, k, h, c=c: land_az.at[way, k, pl.ds(h * 2 * short, 2 * short), columns_of(c)]))
+        s_by.append(Scatter(
+            NY, y, at_y, *ring_sems(9 + 5 * c), lambda r, h, c=c: sums.at[part_b(r, h), columns_of(c)],
+            lambda way, k, h, c=c: land_by.at[way, k, pl.ds(h * 4 * short, 4 * short), columns_of(c)]))
+        s_ay.append(Scatter(
+            NY, y, at_y, *ring_sems(10 + 5 * c), lambda r, h, c=c: sums.at[in_a(near_y(r)), sum_part(c, h)],
+            lambda way, k, h, c=c: land_ay.at[way, k, :, sum_part(c, h)]))
+        s_bz.append(Scatter(
+            NZ, z, at_z, *ring_sems(11 + 5 * c), lambda r, h, c=c: sums.at[in_b(near_z(r)), sum_part(c, h)],
+            lambda way, k, h, c=c: land_bz.at[way, k, :, sum_part(c, h)]))
+        s_x.append(Gather(
+            NX, x, lambda p: device(p, y, z, core), *ring_sems(12 + 5 * c),
+            lambda r, h, c=c: out_ref.at[(x + r + NX) % NX, pl.ds(h * short, short), columns_of(c)]))
+    rings += [a_y, b_z, a_z, b_y, *s_az, *s_by, *s_ay, *s_bz, *s_x]
 
     own_expert = half * 2 + core
     two_expert = half * 2 + other
 
-    def expand(start, size):
-        span, top = pl.ds(start, size), pl.ds(0, size)
+    def experts(start_one, start_two):
+        few_rows = 4 * short
+        one, two = rows(start_one, few_rows), rows(start_two, few_rows)
         tile = 2 * width
 
         @pl.loop(0, 2)
         def _(n):
             columns = rows(n * tile, tile)
-            act[top, columns] = jnp.dot(
-                tok[span, pl.ds(0, features)], enter[:, columns], preferred_element_type=F32
-            )
-
-        gates = tok[span, pl.ds(features, GATES)].astype(F32)
+            both = jnp.concatenate([tok[one, pl.ds(0, features)], tok[two, pl.ds(0, features)]], axis=0)
+            act[:, columns] = jnp.dot(both, enter[:, columns], preferred_element_type=F32)
+
+        gates = jnp.concatenate([tok[one, pl.ds(features, GATES)], tok[two, pl.ds(features, GATES)]], axis=0)
+        gates = gates.astype(F32)
         names = lax.broadcasted_iota(jnp.int32, gates.shape, 1) % 4
         for s, e in ((0, own_expert), (1, two_expert)):
             scale = jnp.sum(jnp.where(names == e, gates, 0.0), axis=-1, keepdims=True)
-            g = act[top, pl.ds(2 * s * width, width)]
-            u = act[top, pl.ds((2 * s + 1) * width, width)]
-            inner[span, pl.ds(s * width, width)] = (g / (1.0 + jnp.exp(-g)) * u * scale).astype(BF16)
-
-    def contract(start, size):
-        span = pl.ds(start, size)
-        tile = features // 2
+            g = act[:, pl.ds(2 * s * width, width)]
+            u = act[:, pl.ds((2 * s + 1) * width, width)]
+            inner[:, pl.ds(s * width, width)] = (g / (1.0 + jnp.exp(-g)) * u * scale).astype(BF16)
 
         @pl.loop(0, 2)
         def _(n):
-            columns = rows(n * tile, tile)
-            sums[span, columns] = jnp.dot(
-                inner[span, :], leave[:, columns], preferred_element_type=F32
-            ).astype(BF16)
-
-    short_phase(a_y, b_z, a_z, b_y)
-    for c in loads[1:]:
-        c.wait()
-    for c in pending[4:]:
-        c.wait_recv()
-    expand(0, 192)
-    a_z.start(2, FIRST)
-    a_z.start(2, SECOND)
-    expand(192, 128)
-    b_y.start(2)
-    a_z.start(3, FIRST)
-    a_z.start(3, SECOND)
-    expand(320, 128)
-    b_y.arrived(1)
-    a_z.start(4)
-    expand(448, 256)
-    contract(448, 256)
-    a_z.arrived(3)
-    expand(704, 128)
-    contract(704, 128)
-    b_y.arrived(2)
-    expand(896, 128)
-    contract(896, 128)
-    s_by.first()
-    a_z.arrived(4)
-    expand(832, 64)
-    contract(832, 64)
-    s_az.first()
-    contract(192, 256)
-    contract(0, 192)
-    s_az.advance(1)
-    s_az.advance(2, FIRST)
-    s_by.advance(1)
-    s_az.advance(2, SECOND)
-    s_az.advance(3, FIRST)
-    s_by.advance(2, FIRST)
-    s_az.advance(3, SECOND)
-    s_az.advance(4, FIRST)
-    s_by.advance(2, SECOND)
-    s_bz.first()
-    s_bz.advance(1)
-    s_az.advance(4, SECOND)
-    s_ay.first()
-    s_bz.advance(2)
-    s_ay.advance(1)
-    s_bz.advance(3)
-    s_ay.advance(2)
-
-    c_x = Gather(NX, x, lambda p: device(p, y, z, core), *ring_sems(12), lambda r, h: mixed.at[
-        (x + r + NX) % NX, pl.ds(h * short, short), :])
-    rings.append(c_x)
-    low, high = pl.ds(0, short), pl.ds(short, short)
-    mixed[x, low, :] = (hidden_ref[low, :] + sums[slot_a, :].astype(F32)).astype(BF16)
-    c_x.hop(1, 0, 0)
-    c_x.hop(1, 0, 1)
-    s_bz.advance(4)
-    mixed[x, high, :] = (hidden_ref[high, :] + sums[slot_b, :].astype(F32)).astype(BF16)
-    c_x.hop(1, 1, 1)
-    c_x.hop(1, 1, 0)
-    out_ref[here, :] = mixed[x]
-    c_x.start(2)
-    c_x.arrived(1)
-    for r in (-1, 1):
-        near = (x + r + NX) % NX
-        out_ref[rows(near * few, few), :] = mixed[near]
-    c_x.arrived(2)
-    near = (x + 2) % NX
-    out_ref[rows(near * few, few), :] = mixed[near]
+            columns = rows(n * cut, cut)
+            result = jnp.dot(inner[...], leave[:, columns], preferred_element_type=F32).astype(BF16)
+            sums[one, columns] = result[:few_rows]
+            sums[two, columns] = result[few_rows:]
+
+    def ready_weights():
+        for c in loads[1:]:
+            c.wait()
+        for c in pending[4:]:
+            c.wait_recv()
+
+    def send_terms(ring_pair, far):
+        def action():
+            for ring in ring_pair:
+                ring.far_terms() if far else ring.near_terms()
+        return action
+
+    def finish(h, c):
+        span = pl.ds(h * short, short)
+        slot = slot_a if h == 0 else slot_b
+        out_ref[x, span, columns_of(c)] = (
+            hidden_ref[span, columns_of(c)] + sums[slot, columns_of(c)].astype(F32)
+        ).astype(BF16)
+        s_x[c].hop(1, h, h)
+        s_x[c].hop(1, h, 1 - h)
+
+    length = 4.3
+    order = interleave(gather_events(a_y, b_z, a_z, b_y, 2.5, 11.0, 5.5), [
+        ("b0", {"bz"}, length, ("u", 128, 192), None),
+        ("a1", {"az1"}, length, ("u", 256, 320), None),
+        ("b1f", {"by1f"}, length, ("u", 512, 704), None),
+        ("a2", {"az2"}, length, ("u", 384, 448), None),
+        ("b1", {"by1"}, length, ("u", 576, 640), send_terms(s_by, False)),
+        ("a3", {"az3"}, length, ("u", 768, 832), send_terms(s_az, False)),
+        ("b2", {"by2"}, length, ("u", 896, 960), send_terms(s_by, True)),
+        ("a4", {"az4"}, length, ("u", 0, 64), send_terms(s_az, True)),
+    ])
+    first_step = next(i for i, item in enumerate(order) if not callable(item))
+    run_in_order(order[:first_step] + [ready_weights] + order[first_step:], {"u": experts})
+
+    events = []
+
+    def at(time, c, name, *actions):
+        def run():
+            for action in actions:
+                action()
+
+        events.append((time, f"{name}_{c}", run))
+
+    for c in range(2):
+        az, by, ay, bz, sx = s_az[c], s_by[c], s_ay[c], s_bz[c], s_x[c]
+        go = lambda ring, k, turn: lambda: ring.advance(k, turn)
+        t = 55.0 + 2.7 * c
+        at(t, c, "az2f", go(az, 2, FIRST))
+        at(t + 5.5, c, "az3f", go(az, 3, FIRST))
+        at(t + 8, c, "az1", go(az, 1, SECOND))
+        at(t + 12, c, "az4f", go(az, 4, FIRST))
+        at(t + 15, c, "az2s", go(az, 2, SECOND))
+        at(t + 20, c, "az3s", go(az, 3, SECOND))
+        at(t + 27, c, "az4s", go(az, 4, SECOND), ay.near_terms, ay.far_terms)
+        at(t + 29, c, "ay2f", go(ay, 2, FIRST))
+        at(t + 29.1, c, "ay1", go(ay, 1, SECOND))
+        at(t + 31, c, "ay2s", go(ay, 2, SECOND), lambda c=c: finish(0, c))
+        t = 52.0 + 5.4 * c
+        at(t, c, "by2f", go(by, 2, FIRST))
+        at(t + 9, c, "by1", go(by, 1, SECOND))
+        at(t + 20, c, "by2s", go(by, 2, SECOND), bz.near_terms, bz.far_terms)
+        at(t + 22, c, "bz2f", go(bz, 2, FIRST))
+        at(t + 22.1, c, "bz1", go(bz, 1, SECOND))
+        at(t + 23.5, c, "bz3f", go(bz, 3, FIRST))
+        at(t + 23.6, c, "bz2s", go(bz, 2, SECOND))
+        at(t + 25, c, "bz4f", go(bz, 4, FIRST))
+        at(t + 25.1, c, "bz3s", go(bz, 3, SECOND))
+        at(t + 27, c, "bz4s", go(bz, 4, SECOND), lambda c=c: finish(1, c))
+        at(90.0 + 3 * c, c, "x2", lambda sx=sx: sx.start(2))
+        at(92.0 + 3 * c, c, "x", lambda sx=sx: (sx.arrived(1), sx.arrived(2)))
+    for action in interleave(events, []):
+        action()
     for c in pending:
         c.wait_send()
     for ring in rings:
@@ -454,19 +474,99 @@
         c.wait_send()
 
 
-def short_phase(a_y, b_z, a_z, b_y):
+def add_into(mine, arrived):
+    step = 16
+
+    @pl.loop(0, mine.shape[0] // step)
+    def _(i):
+        band = rows(i * step, step)
+        mine[band, :] = (mine[band, :].astype(F32) + arrived[band, :].astype(F32)).astype(BF16)
+
+
+def interleave(events, tasks):
+    events, tasks, done, now, order = sorted(events, key=lambda e: e[0]), list(tasks), set(), 0.0, []
+    while events or tasks:
+        ready = [task for task in tasks if done.issuperset(task[1])]
+        if events and (events[0][0] <= now or not ready):
+            time, name, action = events.pop(0)
+            now = max(now, time)
+            order.append(action)
+            done.add(name)
+        else:
+            name, _, length, step, action = ready[0]
+            tasks.remove(ready[0])
+            order += [step] + ([action] if action else [])
+            done.add(name)
+            now += length
+    return order
+
+
+def run_in_order(order, bodies):
+    steps, before = [], [[]]
+    for item in order:
+        if callable(item):
+            before[-1].append(item)
+        else:
+            steps.append(item)
+            before.append([])
+
+    @pl.loop(0, len(steps))
+    def _(s):
+        for i, actions in enumerate(before[:-1]):
+            if actions:
+                @pl.when(s == i)
+                def _():
+                    for action in actions:
+                        action()
+        for kind, body in bodies.items():
+            places = [i for i, step in enumerate(steps) if step[0] == kind]
+            chosen = s == places[0]
+            numbers = [jnp.int32(number) for number in steps[places[0]][1:]]
+            for i in places[1:]:
+                chosen = chosen | (s == i)
+                numbers = [jnp.where(s == i, jnp.int32(new), old) for new, old in zip(steps[i][1:], numbers)]
+            if len(bodies) == 1:
+                body(*numbers)
+            else:
+                pl.when(chosen)(lambda: body(*numbers))
+
+    for action in before[-1]:
+        action()
+
+
+def gather_events(a_y, b_z, a_z, b_y, short_hop, long_start, part):
+    def ready_a():
+        a_y.arrived(1)
+        a_y.arrived(2)
+        a_z.start(1)
+
+    def ready_b():
+        for k in (1, 2, 3, 4):
+            b_z.arrived(k)
+        b_y.start(1)
+
     a_y.start(1)
     b_z.start(1)
-    a_y.start(2)
-    b_z.start(2)
-    a_y.arrived(1)
-    a_y.arrived(2)
-    a_z.start(1)
-    b_z.start(3)
-    b_z.start(4)
-    for k in (1, 2, 3, 4):
-        b_z.arrived(k)
-    b_y.start(1)
+    ta, tb = 2 * short_hop + 0.5, long_start
+    plan = [
+        (short_hop, "ay2", lambda: a_y.start(2)),
+        (short_hop + 0.2, "bz2", lambda: b_z.start(2)),
+        (ta, "ay", ready_a),
+        (tb * 0.55, "bz3", lambda: b_z.start(3)),
+        (tb * 0.8, "bz4", lambda: b_z.start(4)),
+        (tb, "bz", ready_b),
+        (ta + part + 1, "az2f", lambda: a_z.start(2, FIRST)),
+        (ta + 2 * part + 1, "az1", lambda: a_z.start(2, SECOND)),
+        (ta + 3 * part + 1, "az3f", lambda: a_z.start(3, FIRST)),
+        (ta + 4 * part + 1, "az2", lambda: a_z.start(3, SECOND)),
+        (ta + 5 * part + 1, "az4f", lambda: a_z.start(4)),
+        (ta + 6 * part + 1, "az3", lambda: a_z.arrived(3)),
+        (ta + 7 * part + 1, "az4", lambda: a_z.arrived(4)),
+        (tb + 2 * part + 1, "by1f", lambda: b_y.start(2)),
+        (tb + 4 * part + 1, "by1", lambda: b_y.arrived(1)),
+        (tb + 6 * part + 1, "by2", lambda: b_y.arrived(2)),
+    ]
+    return plan
 
 
 def local(
@@ -482,7 +582,7 @@
     plane = NY * NZ * few
     return pl.pallas_call(
         layer_kernel,
-        out_shape=jax.ShapeDtypeStruct((token_count, features), BF16),
+        out_shape=jax.ShapeDtypeStruct((NX, few, features), BF16),
         in_specs=[vmem, hbm] + [vmem] * 4 + [hbm] * 3,
         out_specs=vmem,
         scratch_shapes=[
@@ -496,15 +596,14 @@
             pltpu.VMEM((plane, features + GATES), BF16),
             pltpu.VMEM((features, 4 * width), BF16),
             pltpu.VMEM((2 * width, features), BF16),
-            pltpu.VMEM((256, 4 * width), F32),
-            pltpu.VMEM((plane, 2 * width), BF16),
+            pltpu.VMEM((token_count, 4 * width), F32),
+            pltpu.VMEM((token_count, 2 * width), BF16),
             pltpu.VMEM((plane, features), BF16),
             pltpu.VMEM((2, 4, NY * half, features), BF16),
             pltpu.VMEM((2, 2, NZ * half, features), BF16),
             pltpu.VMEM((2, 2, half, features), BF16),
             pltpu.VMEM((2, 4, half, features), BF16),
-            pltpu.VMEM((NX, few, features), BF16),
-            dma((4,)), dma((7,)), dma((7,)), dma((13, 2, 4, 2)), dma((13, 2, 4, 2)), dma((8,)), dma((8,)),
+            dma((4,)), dma((7,)), dma((7,)), dma((18, 2, 4, 2)), dma((18, 2, 4, 2)), dma((8,)), dma((8,)),
         ],
         compiler_params=pltpu.CompilerParams(
             collective_id=0, has_side_effects=True, vmem_limit_bytes=62 * 2**20
@@ -513,7 +612,7 @@
     )(
         branch_out_proj[0], context, residual, norm_gain.reshape(1, features), router.T, expert_ids.T,
         gate_proj[0], up_proj[0], down_proj[0],
-    )
+    ).reshape(token_count, features)
 
 
 def solution(mesh):

time: 198 us -> 205 us (1.035)
  Pallas kernels: 194 us -> 201 us
    pallas_call x1, Pallas kernels: 194 us -> 201 us  [local(): pl.pallas_call(layer_kernel, out_shape=jax.ShapeDtypeStruct((NX, few, fea...]
where the time goes in v3:
time: 205 us; the launch traced here: 204 us
  Pallas kernels  201 us (98%)
  local copies, waits for them, and re-layouts  3.6 us (2%)
    pallas_call x1, Pallas kernels, local(): pl.pallas_call(layer_kernel, out_shape=jax.ShapeDtypeStruct((NX, few, fea...  201 us

profile of v3, /device:TPU:8, one launch (start us, length us, event | category | flops | bytes accessed | tf_op | source)
XLA Modules:
  0.0 204.4 jit_solution(2304191165743507777)
XLA Ops:
  0.0 1.3 reshape.6.gain_ref
  1.3 200.7 %layer.1 = bf16[4,32,4096]{2,1,0:T(8,128)(2,1)} custom-call(bf16[256,1024]{1,0:T(8,128)(2,1)} %bitcast.11, bf16[128,4096]{1,0:T(8,128)(2,1)} %context_ref.1, bf16[128,4096]{1,0:T(8,128)(2,1)} %residual_ref.1, bf16[1,4096]{1,0:T(2,128)(2,1)} %reshape.6.gain_ref, bf16[4,4096]{1,0:T(4,128)(2,1)} %bitcast.12, s32[2,128]{1,0:T(2,128)} %bitcast.13, ...), custom_call_target="tpu_custom_call" | custom-call | tf_op jit(solution)/shard_map/layer/pallas_call | solution.py:583
  202.1 2.3 %copy.11 = bf16[128,4096]{1,0:T(8,128)(2,1)} copy(bf16[128,4096]{1,0:T(8,128)(2,1)} %bitcast.7) | data formatting | bytes 2097152

commit v4 on v3

--- a/solution.py
+++ b/solution.py
@@ -108,6 +108,10 @@
     def far_terms(self):
         for way in (0, 1):
             self.put(1, way, way)
+
+    def first_terms(self):
+        self.far_terms()
+        self.near_terms()
 
     def advance(self, k, turn=None):
         for t in (FIRST, SECOND) if turn is None else (turn,):
@@ -241,7 +245,7 @@
         loads[0].wait()
         pending[3].wait_recv()
 
-    order = interleave(gather_events(a_y, b_z, a_z, b_y, 1.8, 7.0, 2.7), [
+    order = interleave(gather_events(a_y, b_z, a_z, b_y, 2.0, 9.0, 2.9), [
         ("a0", {"ay"}, 0.5, ("a", 0), None),
         ("b0", {"bz"}, 0.8, ("b", 0), None),
         ("a1m", {"az1"}, 0.5, ("a", -1), None),
@@ -295,7 +299,7 @@
     logits = jnp.zeros((few, 4), F32)
     for j in range(2 * NX):
         columns = pl.ds(j * wide, wide)
-        normed = (hidden_ref[:, columns] * inv_rms * gain_ref[:, columns].astype(F32)).astype(BF16)
+        normed = (hidden_ref[:, columns] * inv_rms * gain_ref[columns].astype(F32)[None, :]).astype(BF16)
         tok[slot_a, columns] = normed[:short]
         tok[slot_b, columns] = normed[short:]
         logits = logits + lax.dot_general(
@@ -330,11 +334,8 @@
     def token_part(h):
         return pl.ds(0, cut) if h == 0 else pl.ds(cut, cut + GATES)
 
-    def columns_of(c):
-        return pl.ds(c * cut, cut)
-
-    def sum_part(c, h):
-        return pl.ds(c * cut + h * (cut // 2), cut // 2)
+    def sum_part(h):
+        return pl.ds(h * cut, cut)
 
     in_a = lambda p: rows(A_ROWS[0] + p * short, short)
     in_b = lambda p: rows(B_ROWS[0] + p * short, short)
@@ -344,24 +345,17 @@
     b_z = Gather(NZ, z, at_z, *ring_sems(5), lambda r, h: tok.at[in_b(near_z(r)), token_part(h)])
     a_z = Gather(NZ, z, at_z, *ring_sems(6), lambda r, h: tok.at[part_a(r, h), :], True)
     b_y = Gather(NY, y, at_y, *ring_sems(7), lambda r, h: tok.at[part_b(r, h), :], True)
-    s_az, s_by, s_ay, s_bz, s_x = [], [], [], [], []
-    for c in range(2):
-        s_az.append(Scatter(
-            NZ, z, at_z, *ring_sems(8 + 5 * c), lambda r, h, c=c: sums.at[part_a(r, h), columns_of(c)],
-            lambda way, k, h, c=c: land_az.at[way, k, pl.ds(h * 2 * short, 2 * short), columns_of(c)]))
-        s_by.append(Scatter(
-            NY, y, at_y, *ring_sems(9 + 5 * c), lambda r, h, c=c: sums.at[part_b(r, h), columns_of(c)],
-            lambda way, k, h, c=c: land_by.at[way, k, pl.ds(h * 4 * short, 4 * short), columns_of(c)]))
-        s_ay.append(Scatter(
-            NY, y, at_y, *ring_sems(10 + 5 * c), lambda r, h, c=c: sums.at[in_a(near_y(r)), sum_part(c, h)],
-            lambda way, k, h, c=c: land_ay.at[way, k, :, sum_part(c, h)]))
-        s_bz.append(Scatter(
-            NZ, z, at_z, *ring_sems(11 + 5 * c), lambda r, h, c=c: sums.at[in_b(near_z(r)), sum_part(c, h)],
-            lambda way, k, h, c=c: land_bz.at[way, k, :, sum_part(c, h)]))
-        s_x.append(Gather(
-            NX, x, lambda p: device(p, y, z, core), *ring_sems(12 + 5 * c),
-            lambda r, h, c=c: out_ref.at[(x + r + NX) % NX, pl.ds(h * short, short), columns_of(c)]))
-    rings += [a_y, b_z, a_z, b_y, *s_az, *s_by, *s_ay, *s_bz, *s_x]
+    s_az = Scatter(NZ, z, at_z, *ring_sems(8), lambda r, h: sums.at[part_a(r, h), :],
+                   lambda way, k, h: land_az.at[way, k, pl.ds(h * 2 * short, 2 * short), :])
+    s_by = Scatter(NY, y, at_y, *ring_sems(9), lambda r, h: sums.at[part_b(r, h), :],
+                   lambda way, k, h: land_by.at[way, k, pl.ds(h * 4 * short, 4 * short), :])
+    s_ay = Scatter(NY, y, at_y, *ring_sems(10), lambda r, h: sums.at[in_a(near_y(r)), sum_part(h)],
+                   lambda way, k, h: land_ay.at[way, k, :, sum_part(h)])
+    s_bz = Scatter(NZ, z, at_z, *ring_sems(11), lambda r, h: sums.at[in_b(near_z(r)), sum_part(h)],
+                   lambda way, k, h: land_bz.at[way, k, :, sum_part(h)])
+    s_x = Gather(NX, x, lambda p: device(p, y, z, core), *ring_sems(12), lambda r, h: out_ref.at[
+        (x + r + NX) % NX, pl.ds(h * short, short), :])
+    rings += [a_y, b_z, a_z, b_y, s_az, s_by, s_ay, s_bz, s_x]
 
     own_expert = half * 2 + core
     two_expert = half * 2 + other
@@ -399,73 +393,53 @@
         for c in pending[4:]:
             c.wait_recv()
 
-    def send_terms(ring_pair, far):
-        def action():
-            for ring in ring_pair:
-                ring.far_terms() if far else ring.near_terms()
-        return action
-
-    def finish(h, c):
+    def finish(h):
         span = pl.ds(h * short, short)
         slot = slot_a if h == 0 else slot_b
-        out_ref[x, span, columns_of(c)] = (
-            hidden_ref[span, columns_of(c)] + sums[slot, columns_of(c)].astype(F32)
-        ).astype(BF16)
-        s_x[c].hop(1, h, h)
-        s_x[c].hop(1, h, 1 - h)
+        out_ref[x, span, :] = (hidden_ref[span, :] + sums[slot, :].astype(F32)).astype(BF16)
+        s_x.hop(1, h, h)
+        s_x.hop(1, h, 1 - h)
 
     length = 4.3
-    order = interleave(gather_events(a_y, b_z, a_z, b_y, 2.5, 11.0, 5.5), [
+    events = gather_events(a_y, b_z, a_z, b_y, 3.0, 14.5, 6.0)
+
+    order = interleave(events, [
         ("b0", {"bz"}, length, ("u", 128, 192), None),
         ("a1", {"az1"}, length, ("u", 256, 320), None),
         ("b1f", {"by1f"}, length, ("u", 512, 704), None),
         ("a2", {"az2"}, length, ("u", 384, 448), None),
-        ("b1", {"by1"}, length, ("u", 576, 640), send_terms(s_by, False)),
-        ("a3", {"az3"}, length, ("u", 768, 832), send_terms(s_az, False)),
-        ("b2", {"by2"}, length, ("u", 896, 960), send_terms(s_by, True)),
-        ("a4", {"az4"}, length, ("u", 0, 64), send_terms(s_az, True)),
+        ("b1", {"by1"}, length, ("u", 576, 640), None),
+        ("a3", {"az3"}, length, ("u", 768, 832), None),
+        ("b2", {"by2", "a3", "b1"}, length, ("u", 896, 960), s_by.first_terms),
+        ("a4", {"az4", "b2"}, length, ("u", 0, 64), s_az.first_terms),
     ])
     first_step = next(i for i, item in enumerate(order) if not callable(item))
     run_in_order(order[:first_step] + [ready_weights] + order[first_step:], {"u": experts})
-
-    events = []
-
-    def at(time, c, name, *actions):
-        def run():
-            for action in actions:
-                action()
-
-        events.append((time, f"{name}_{c}", run))
-
-    for c in range(2):
-        az, by, ay, bz, sx = s_az[c], s_by[c], s_ay[c], s_bz[c], s_x[c]
-        go = lambda ring, k, turn: lambda: ring.advance(k, turn)
-        t = 55.0 + 2.7 * c
-        at(t, c, "az2f", go(az, 2, FIRST))
-        at(t + 5.5, c, "az3f", go(az, 3, FIRST))
-        at(t + 8, c, "az1", go(az, 1, SECOND))
-        at(t + 12, c, "az4f", go(az, 4, FIRST))
-        at(t + 15, c, "az2s", go(az, 2, SECOND))
-        at(t + 20, c, "az3s", go(az, 3, SECOND))
-        at(t + 27, c, "az4s", go(az, 4, SECOND), ay.near_terms, ay.far_terms)
-        at(t + 29, c, "ay2f", go(ay, 2, FIRST))
-        at(t + 29.1, c, "ay1", go(ay, 1, SECOND))
-        at(t + 31, c, "ay2s", go(ay, 2, SECOND), lambda c=c: finish(0, c))
-        t = 52.0 + 5.4 * c
-        at(t, c, "by2f", go(by, 2, FIRST))
-        at(t + 9, c, "by1", go(by, 1, SECOND))
-        at(t + 20, c, "by2s", go(by, 2, SECOND), bz.near_terms, bz.far_terms)
-        at(t + 22, c, "bz2f", go(bz, 2, FIRST))
-        at(t + 22.1, c, "bz1", go(bz, 1, SECOND))
-        at(t + 23.5, c, "bz3f", go(bz, 3, FIRST))
-        at(t + 23.6, c, "bz2s", go(bz, 2, SECOND))
-        at(t + 25, c, "bz4f", go(bz, 4, FIRST))
-        at(t + 25.1, c, "bz3s", go(bz, 3, SECOND))
-        at(t + 27, c, "bz4s", go(bz, 4, SECOND), lambda c=c: finish(1, c))
-        at(90.0 + 3 * c, c, "x2", lambda sx=sx: sx.start(2))
-        at(92.0 + 3 * c, c, "x", lambda sx=sx: (sx.arrived(1), sx.arrived(2)))
-    for action in interleave(events, []):
-        action()
+    s_az.advance(1)
+    s_az.advance(2, FIRST)
+    s_by.advance(1)
+    s_az.advance(2, SECOND)
+    s_az.advance(3, FIRST)
+    s_by.advance(2, FIRST)
+    s_az.advance(3, SECOND)
+    s_az.advance(4, FIRST)
+
+
+    s_by.advance(2, SECOND)
+    s_bz.first_terms()
+    s_bz.advance(1)
+    s_bz.advance(2)
+    s_az.advance(4, SECOND)
+    s_ay.first_terms()
+    s_bz.advance(3)
+    s_ay.advance(1)
+    s_bz.advance(4)
+    finish(1)
+    s_ay.advance(2)
+    finish(0)
+    s_x.start(2)
+    s_x.arrived(1)
+    s_x.arrived(2)
     for c in pending:
         c.wait_send()
     for ring in rings:
@@ -538,33 +512,34 @@
     def ready_a():
         a_y.arrived(1)
         a_y.arrived(2)
-        a_z.start(1)
+        b_z.start(3)
+        a_z.start(1, FIRST)
 
     def ready_b():
         for k in (1, 2, 3, 4):
             b_z.arrived(k)
         b_y.start(1)
+        a_z.start(1, SECOND)
 
     a_y.start(1)
     b_z.start(1)
-    ta, tb = 2 * short_hop + 0.5, long_start
+    late = long_start + 1
     plan = [
         (short_hop, "ay2", lambda: a_y.start(2)),
         (short_hop + 0.2, "bz2", lambda: b_z.start(2)),
-        (ta, "ay", ready_a),
-        (tb * 0.55, "bz3", lambda: b_z.start(3)),
-        (tb * 0.8, "bz4", lambda: b_z.start(4)),
-        (tb, "bz", ready_b),
-        (ta + part + 1, "az2f", lambda: a_z.start(2, FIRST)),
-        (ta + 2 * part + 1, "az1", lambda: a_z.start(2, SECOND)),
-        (ta + 3 * part + 1, "az3f", lambda: a_z.start(3, FIRST)),
-        (ta + 4 * part + 1, "az2", lambda: a_z.start(3, SECOND)),
-        (ta + 5 * part + 1, "az4f", lambda: a_z.start(4)),
-        (ta + 6 * part + 1, "az3", lambda: a_z.arrived(3)),
-        (ta + 7 * part + 1, "az4", lambda: a_z.arrived(4)),
-        (tb + 2 * part + 1, "by1f", lambda: b_y.start(2)),
-        (tb + 4 * part + 1, "by1", lambda: b_y.arrived(1)),
-        (tb + 6 * part + 1, "by2", lambda: b_y.arrived(2)),
+        (2 * short_hop + 0.5, "ay", ready_a),
+        (long_start * 0.8, "bz4", lambda: b_z.start(4)),
+        (long_start, "bz", ready_b),
+        (late, "az2f", lambda: a_z.start(2, FIRST)),
+        (late + part, "az1", lambda: a_z.start(2, SECOND)),
+        (late + 2 * part, "az3f", lambda: a_z.start(3, FIRST)),
+        (late + 3 * part, "az2", lambda: a_z.start(3, SECOND)),
+        (late + 4 * part, "az4f", lambda: a_z.start(4)),
+        (late + 5 * part, "az3", lambda: a_z.arrived(3)),
+        (late + 6 * part, "az4", lambda: a_z.arrived(4)),
+        (long_start + 2 * part, "by1f", lambda: b_y.start(2)),
+        (long_start + 4 * part, "by1", lambda: b_y.arrived(1)),
+        (long_start + 6 * part, "by2", lambda: b_y.arrived(2)),
     ]
     return plan
 
@@ -603,14 +578,14 @@
             pltpu.VMEM((2, 2, NZ * half, features), BF16),
             pltpu.VMEM((2, 2, half, features), BF16),
             pltpu.VMEM((2, 4, half, features), BF16),
-            dma((4,)), dma((7,)), dma((7,)), dma((18, 2, 4, 2)), dma((18, 2, 4, 2)), dma((8,)), dma((8,)),
+            dma((4,)), dma((7,)), dma((7,)), dma((13, 2, 4, 2)), dma((13, 2, 4, 2)), dma((8,)), dma((8,)),
         ],
         compiler_params=pltpu.CompilerParams(
             collective_id=0, has_side_effects=True, vmem_limit_bytes=62 * 2**20
         ),
         name="layer",
     )(
-        branch_out_proj[0], context, residual, norm_gain.reshape(1, features), router.T, expert_ids.T,
+        branch_out_proj[0], context, residual, norm_gain, router.T, expert_ids.T,
         gate_proj[0], up_proj[0], down_proj[0],
     ).reshape(token_count, features)
 

time: 205 us -> 190 us (0.927)
  Pallas kernels: 201 us -> 188 us
    pallas_call x1, Pallas kernels: 201 us -> 188 us  [local(): pl.pallas_call(layer_kernel, out_shape=jax.ShapeDtypeStruct((NX, few, fea...]
where the time goes in v4:
time: 190 us
  Pallas kernels  188 us (99%)
  local copies, waits for them, and re-layouts  2.29 us (1%)
    pallas_call x1, Pallas kernels, local(): pl.pallas_call(layer_kernel, out_shape=jax.ShapeDtypeStruct((NX, few, fea...  188 us

profile of v4, /device:TPU:8, one launch (start us, length us, event | category | flops | bytes accessed | tf_op | source)
XLA Modules:
  0.0 189.9 jit_solution(15057602262444243386)
XLA Ops:
  0.0 187.6 %layer.1 = bf16[4,32,4096]{2,1,0:T(8,128)(2,1)} custom-call(bf16[256,1024]{1,0:T(8,128)(2,1)} %bitcast.11, bf16[128,4096]{1,0:T(8,128)(2,1)} %context_ref.1, bf16[128,4096]{1,0:T(8,128)(2,1)} %residual_ref.1, bf16[4096]{0:T(1024)(128)(2,1)} %gain_ref.1, bf16[4,4096]{1,0:T(4,128)(2,1)} %bitcast.12, s32[2,128]{1,0:T(2,128)} %bitcast.13, ...), custom_call_target="tpu_custom_call" | custom-call | tf_op jit(solution)/shard_map/layer/pallas_call | solution.py:558
  187.6 2.3 %copy.11 = bf16[128,4096]{1,0:T(8,128)(2,1)} copy(bf16[128,4096]{1,0:T(8,128)(2,1)} %bitcast.7) | data formatting | bytes 2097152

commit v5 on v4

--- a/solution.py
+++ b/solution.py
@@ -191,7 +191,7 @@
     pending.append(pair_copy(4, gate_ref, enter.at[:, pl.ds(2 * width, width)], sibling))
     pending.append(pair_copy(5, up_ref, enter.at[:, pl.ds(3 * width, width)], sibling))
     pending.append(pair_copy(6, down_ref, leave.at[pl.ds(width, width), :], sibling))
-    for c in pending[:4]:
+    for c in (pending[1], pending[2], pending[0], pending[3]):
         c.start()
     for c in pending[:3]:
         c.wait_recv()
@@ -403,6 +403,7 @@
     length = 4.3
     events = gather_events(a_y, b_z, a_z, b_y, 3.0, 14.5, 6.0)
 
+    events.append((max(time for time, _, _ in events) + 5.0, "near", s_az.near_terms))
     order = interleave(events, [
         ("b0", {"bz"}, length, ("u", 128, 192), None),
         ("a1", {"az1"}, length, ("u", 256, 320), None),
@@ -411,12 +412,12 @@
         ("b1", {"by1"}, length, ("u", 576, 640), None),
         ("a3", {"az3"}, length, ("u", 768, 832), None),
         ("b2", {"by2", "a3", "b1"}, length, ("u", 896, 960), s_by.first_terms),
-        ("a4", {"az4", "b2"}, length, ("u", 0, 64), s_az.first_terms),
+        ("a4", {"near", "b2"}, length, ("u", 0, 64), s_az.far_terms),
     ])
     first_step = next(i for i, item in enumerate(order) if not callable(item))
     run_in_order(order[:first_step] + [ready_weights] + order[first_step:], {"u": experts})
+    s_az.advance(2, FIRST)
     s_az.advance(1)
-    s_az.advance(2, FIRST)
     s_by.advance(1)
     s_az.advance(2, SECOND)
     s_az.advance(3, FIRST)

time: 190 us -> 187 us (0.984)
  Pallas kernels: 188 us -> 185 us
    pallas_call x1, Pallas kernels: 188 us -> 185 us  [local(): pl.pallas_call(layer_kernel, out_shape=jax.ShapeDtypeStruct((NX, few, fea...]
where the time goes in v5:
time: 187 us
  Pallas kernels  185 us (99%)
  local copies, waits for them, and re-layouts  2.29 us (1%)
    pallas_call x1, Pallas kernels, local(): pl.pallas_call(layer_kernel, out_shape=jax.ShapeDtypeStruct((NX, few, fea...  185 us

profile of v5, /device:TPU:8, one launch (start us, length us, event | category | flops | bytes accessed | tf_op | source)
XLA Modules:
  0.0 186.9 jit_solution(5989570365851436582)
XLA Ops:
  0.0 184.6 %layer.1 = bf16[4,32,4096]{2,1,0:T(8,128)(2,1)} custom-call(bf16[256,1024]{1,0:T(8,128)(2,1)} %bitcast.11, bf16[128,4096]{1,0:T(8,128)(2,1)} %context_ref.1, bf16[128,4096]{1,0:T(8,128)(2,1)} %residual_ref.1, bf16[4096]{0:T(1024)(128)(2,1)} %gain_ref.1, bf16[4,4096]{1,0:T(4,128)(2,1)} %bitcast.12, s32[2,128]{1,0:T(2,128)} %bitcast.13, ...), custom_call_target="tpu_custom_call" | custom-call | tf_op jit(solution)/shard_map/layer/pallas_call | solution.py:559
  184.6 2.3 %copy.11 = bf16[128,4096]{1,0:T(8,128)(2,1)} copy(bf16[128,4096]{1,0:T(8,128)(2,1)} %bitcast.7) | data formatting | bytes 2097152
